TPU v7x, 32 devices: a whole 2x2x4 slice. The times are simulated.
32 devices in a mesh: dp: 8 (over z, y), tensor: 4 (over x, core).
Axes of the slice: x: 2, y: 2, z: 4, core: 2. Of those that a mesh axis runs over, the one named last changes fastest.
Arguments:
- tokens: bfloat16 [32768, 768], P('dp'), may hold values from -6 to 6
- lengths: int32 [32], P('dp'), may hold values from 128 to 1024, as said below
- tie_map: int32 [4], replicated, may hold values from 0 to 3, as said below
- norm_gains: bfloat16 [4, 2, 768], P(None, None, ('dp', 'tensor')), may hold values from 0.25 to 1.75
- bias_rows: bfloat16 [4, 10, 768], P(None, None, ('dp', 'tensor')), may hold values from -2 to 2
- attention_in: bfloat16 [4, 3, 768, 768], P(None, None, 'dp', 'tensor'), may hold values from -0.3125 to 0.3125
- attention_out: bfloat16 [4, 768, 768], P(None, 'tensor', 'dp'), may hold values from -0.875 to 0.875
- expand_weight: bfloat16 [4, 768, 3072], P(None, 'dp', 'tensor'), may hold values from -0.21875 to 0.21875
- project_weight: bfloat16 [4, 3072, 768], P(None, 'tensor', 'dp'), may hold values from -0.109375 to 0.109375
- cotangent: bfloat16 [32768, 768], P('dp'), may hold values from -6 to 6
Outputs:
- layer_out: bfloat16 [32768, 768], P('dp')
- tokens_grad: bfloat16 [32768, 768], P('dp')
- gains_grad: float32 [4, 2, 768], P(None, None, ('dp', 'tensor'))
- bias_grad: float32 [4, 10, 768], P(None, None, ('dp', 'tensor'))
- attention_in_grad: float32 [4, 3, 768, 768], P(None, None, 'dp', 'tensor')
- attention_out_grad: float32 [4, 768, 768], P(None, 'tensor', 'dp')
- expand_grad: float32 [4, 768, 3072], P(None, 'dp', 'tensor')
- project_grad: float32 [4, 3072, 768], P(None, 'tensor', 'dp')
Inputs may be any that keep to these rules, and one draw needn't show every extreme that they name: `lengths`: the live tokens of a slot come first in it, the rest is padding. `tie_map`: kind 0: first norm, query, key and value projections with their biases; kind 1: attention output projection and bias; kind 2: second norm, first feed-forward matrix and bias; kind 3: second feed-forward matrix and bias. Every source is named by some kind.
All inputs are finite; a program needn't handle non-finite values.
Results may differ from a plain program's by a relative error of at most 0.019.
Values may be sent and summed in bfloat16 or wider, within the bound.
A program may use at most 192 MiB of HBM per device.

v0:
```python
import jax
import jax.numpy as jnp
from jax import lax
from jax.experimental import pallas as pl
from jax.experimental.pallas import tpu as pltpu
from jax.sharding import PartitionSpec as P

D = 768
HEAD_DIM = 64
FF = 3072
NSRC = 4
EPS = 1e-05
MASKED = -1e30
F32 = jnp.float32
BF16 = jnp.bfloat16
VMEM_LIMIT = 60 * 1024 * 1024


def dot_nn(a, b):
    return lax.dot_general(a, b, (((1,), (0,)), ((), ())), preferred_element_type=F32)


def dot_nt(a, b):
    return lax.dot_general(a, b, (((1,), (1,)), ((), ())), preferred_element_type=F32)


def norm_parts(v):
    center = jnp.mean(v, -1, keepdims=True)
    centered = v - center
    r = lax.rsqrt(jnp.mean(centered * centered, -1, keepdims=True) + EPS)
    return centered * r, r


def head_mask(shape, h):
    lane = lax.broadcasted_iota(jnp.int32, shape, 1)
    return (lane >= h * HEAD_DIM) & (lane < (h + 1) * HEAD_DIM)


def blocks(total, size):
    return [slice(i * size, (i + 1) * size) for i in range(total // size)]


def attention_forward(
    len_ref, x_ref, g_ref, rows_ref, bqv_ref,
    q_ref, v_ref, kt_ref, p_ref, o_ref, a1t_ref, h1_ref, a2_ref, a2t_ref,
    a1_ref, k_ref, vt_ref, ot_ref, attn_ref,
):
    t = pl.program_id(0)
    n = x_ref.shape[0]
    width = g_ref.shape[-1]
    heads = width // HEAD_DIM
    step = 256
    length = len_ref[0]

    @pl.when(t == 0)
    def _():
        @pl.loop(0, n // step)
        def _(b):
            rows = pl.ds(pl.multiple_of(b * step, step), step)
            xhat, _ = norm_parts(x_ref[rows, :].astype(F32))
            a1 = xhat * rows_ref[0:1, :] + rows_ref[2:3, :]
            a1_ref[rows, :] = a1.astype(BF16)
            a1t_ref[:, rows] = a1.astype(BF16).T
            attn_ref[rows, :] = x_ref[rows, :].astype(F32) + rows_ref[5:6, :]

    @pl.loop(0, n // step)
    def _(b):
        rows = pl.ds(pl.multiple_of(b * step, step), step)
        a1 = a1_ref[rows, :]
        q = (dot_nn(a1, g_ref[0, 0]) + bqv_ref[0, 0:1, :]).astype(BF16)
        q_ref[0, rows, :] = q * jnp.asarray(HEAD_DIM ** -0.5, BF16)
        k = dot_nn(a1, g_ref[0, 1]).astype(BF16)
        k_ref[rows, :] = k
        kt_ref[0, :, rows] = k.T
        v = (dot_nn(a1, g_ref[0, 2]) + bqv_ref[0, 1:2, :]).astype(BF16)
        v_ref[0, rows, :] = v
        vt_ref[:, rows] = v.T

    for h in range(heads):
        k = k_ref[...]
        k = jnp.where(head_mask(k.shape, h), k, jnp.zeros_like(k))
        for b in range(n // step):
            first, last = b * step, (b + 1) * step
            q = q_ref[0, first:last, :]
            key = lax.broadcasted_iota(jnp.int32, (last, step), 0)
            query = lax.broadcasted_iota(jnp.int32, (step, step), 1) + first
            s = dot_nt(k[:last], q)
            near = jnp.where(
                (key[first:] <= query) & (key[first:] < length), s[first:], MASKED
            )
            if b:
                far = jnp.where(key[:first] < length, s[:first], MASKED)
                top = jnp.maximum(
                    jnp.max(far, 0, keepdims=True), jnp.max(near, 0, keepdims=True)
                )
                e_far = jnp.exp(far - top)
                e_near = jnp.exp(near - top)
                total = jnp.sum(e_far, 0, keepdims=True) + jnp.sum(e_near, 0, keepdims=True)
                scale = 1.0 / total
                p_ref[0, h, :first, first:last] = (e_far * scale).astype(BF16)
            else:
                top = jnp.max(near, 0, keepdims=True)
                e_near = jnp.exp(near - top)
                scale = 1.0 / jnp.sum(e_near, 0, keepdims=True)
            p_ref[0, h, first:last, first:last] = (e_near * scale).astype(BF16)
            ot_ref[h * HEAD_DIM : (h + 1) * HEAD_DIM, first:last] = dot_nn(
                vt_ref[h * HEAD_DIM : (h + 1) * HEAD_DIM, :last],
                p_ref[0, h, :last, first:last],
            ).astype(BF16)

    @pl.loop(0, n // step)
    def _(b):
        rows = pl.ds(pl.multiple_of(b * step, step), step)
        o = ot_ref[:, rows].T
        o_ref[0, rows, :] = o
        attn_ref[rows, :] += dot_nt(o, g_ref[0, 3])

    @pl.when(t == pl.num_programs(0) - 1)
    def _():
        @pl.loop(0, n // step)
        def _(b):
            rows = pl.ds(pl.multiple_of(b * step, step), step)
            h1 = attn_ref[rows, :]
            h1_ref[rows, :] = h1
            xhat, _ = norm_parts(h1)
            a2 = (xhat * rows_ref[1:2, :] + rows_ref[6:7, :]).astype(BF16)
            a2_ref[rows, :] = a2
            a2t_ref[:, rows] = a2.T


SQRT_2_PI = 0.7978845608028654


def feed_forward_both(
    len_ref, c_ref, a2_ref, a2t_ref, h1_ref, w1_ref, w2_ref, rows_ref,
    out_ref, d1_ref, d2_ref, dh1_ref, gb_ref, gbt_ref, sums_ref,
    gf_ref, gft_ref, feed_ref, da2_ref, h_ref, df_ref,
):
    t = pl.program_id(0)
    n = c_ref.shape[0]
    step = 256
    length = len_ref[0]

    @pl.when(t == 0)
    def _():
        sums_ref[...] = jnp.zeros_like(sums_ref)

        @pl.loop(0, n // step)
        def _(b):
            rows = pl.ds(pl.multiple_of(b * step, step), step)
            place = b * step + lax.broadcasted_iota(jnp.int32, (step, 1), 0)
            live = (place < length).astype(F32)
            g = (c_ref[rows, :].astype(F32) * live).astype(BF16)
            gf_ref[rows, :] = g
            gft_ref[:, rows] = g.T
            sums_ref[7:8, :] += jnp.sum(g.astype(F32), 0, keepdims=True)

    bias = rows_ref[pl.ds(8 + t, 1), :]

    @pl.loop(0, n // step)
    def _(b):
        rows = pl.ds(pl.multiple_of(b * step, step), step)
        f = dot_nn(a2_ref[rows, :], w1_ref[0]) + bias
        dh = dot_nn(gf_ref[rows, :], w2_ref[0])
        f2 = f * f
        th = jnp.tanh(f * (SQRT_2_PI + (SQRT_2_PI * 0.044715) * f2))
        half = 0.5 + 0.5 * th
        h = (f * half).astype(BF16)
        slope = half + f * (0.5 - 0.5 * th * th) * (
            SQRT_2_PI + (3 * SQRT_2_PI * 0.044715) * f2
        )
        df = (dh * slope).astype(BF16)
        h_ref[rows, :] = h
        df_ref[rows, :] = df
        sums_ref[pl.ds(8 + t, 1), :] += jnp.sum(df.astype(F32), 0, keepdims=True)
        feed = dot_nt(h, w2_ref[0])
        da2 = dot_nt(df, w1_ref[0])

        @pl.when(t == 0)
        def _():
            feed_ref[rows, :] = feed
            da2_ref[rows, :] = da2

        @pl.when(t > 0)
        def _():
            feed_ref[rows, :] += feed
            da2_ref[rows, :] += da2

    @pl.loop(0, D // step)
    def _(b):
        rows = pl.ds(pl.multiple_of(b * step, step), step)
        d1_ref[0, rows, :] = dot_nn(a2t_ref[rows, :], df_ref[...]).astype(BF16)
        d2_ref[0, rows, :] = dot_nn(gft_ref[rows, :], h_ref[...]).astype(BF16)

    @pl.when(t == pl.num_programs(0) - 1)
    def _():
        @pl.loop(0, n // step)
        def _(b):
            rows = pl.ds(pl.multiple_of(b * step, step), step)
            place = b * step + lax.broadcasted_iota(jnp.int32, (step, 1), 0)
            live = (place < length).astype(F32)
            h1 = h1_ref[rows, :]
            out_ref[rows, :] = (live * (h1 + (feed_ref[rows, :] + rows_ref[7:8, :]))).astype(BF16)
            xhat, r = norm_parts(h1)
            da2 = da2_ref[rows, :]
            sums_ref[1:2, :] += jnp.sum(da2 * xhat, 0, keepdims=True)
            sums_ref[6:7, :] += jnp.sum(da2, 0, keepdims=True)
            dg = da2 * rows_ref[1:2, :]
            dv = r * (
                dg
                - jnp.mean(dg, -1, keepdims=True)
                - xhat * jnp.mean(dg * xhat, -1, keepdims=True)
            )
            dh1 = live * c_ref[rows, :].astype(F32) + dv
            dh1_ref[rows, :] = dh1
            gb = dh1.astype(BF16)
            gb_ref[rows, :] = gb
            gbt_ref[:, rows] = gb.T
            sums_ref[5:6, :] += jnp.sum(gb.astype(F32), 0, keepdims=True)


def attention_backward(
    x_ref, g_ref, rows_ref, dh1_ref, gb_ref, gbt_ref, q_ref, v_ref, kt_ref, p_ref,
    o_ref, a1t_ref,
    d0_ref, xg_ref, sums_ref, bqv_ref,
    do_ref, delta_ref, dqt_ref, dq_ref, dk_ref, dv_ref, da1_ref,
):
    t = pl.program_id(0)
    n = x_ref.shape[0]
    width = g_ref.shape[-1]
    heads = width // HEAD_DIM
    step = 256
    pick = (
        lax.broadcasted_iota(jnp.int32, (16, width), 1) // HEAD_DIM
        == lax.broadcasted_iota(jnp.int32, (16, width), 0)
    ).astype(BF16)

    @pl.loop(0, n // step)
    def _(b):
        rows = pl.ds(pl.multiple_of(b * step, step), step)
        do = dot_nn(gb_ref[rows, :], g_ref[0, 3]).astype(BF16)
        do_ref[rows, :] = do
        prod = do.astype(F32) * o_ref[0, rows, :].astype(F32)
        high = prod.astype(BF16)
        low = (prod - high.astype(F32)).astype(BF16)
        delta_ref[:, rows] = dot_nt(pick, high) + dot_nt(pick, low)

    dqt_ref[...] = jnp.zeros_like(dqt_ref)
    for b in range(n // step):
        first, last = b * step, (b + 1) * step
        do = do_ref[first:, :]
        q = q_ref[0, first:, :]
        v = v_ref[0, first:last, :]
        dk, dv = None, None
        for h in range(heads):
            mine = head_mask((1, width), h)
            zero = jnp.zeros((), BF16)
            p = p_ref[0, h, first:last, first:]
            dp = dot_nt(jnp.where(mine, v, zero), do)
            ds = (p.astype(F32) * (dp - delta_ref[h : h + 1, first:])).astype(BF16)
            part = dot_nn(p, jnp.where(mine, do, zero))
            dv = part if dv is None else dv + part
            part = dot_nn(ds, jnp.where(mine, q, zero))
            dk = part if dk is None else dk + part
            head = slice(h * HEAD_DIM, (h + 1) * HEAD_DIM)
            dqt_ref[head, first:] += dot_nn(kt_ref[0, head, first:last], ds)
        dk_ref[first:last, :] = dk.astype(BF16)
        dv_ref[first:last, :] = dv.astype(BF16)

    @pl.when(t == 0)
    def _():
        da1_ref[...] = jnp.zeros_like(da1_ref)

    bqv_ref[...] = jnp.zeros_like(bqv_ref)

    @pl.loop(0, n // step)
    def _(b):
        rows = pl.ds(pl.multiple_of(b * step, step), step)
        dq = (dqt_ref[:, rows] * HEAD_DIM ** -0.5).astype(BF16).T
        dk = dk_ref[rows, :]
        dv = dv_ref[rows, :]
        dq_ref[rows, :] = dq
        bqv_ref[0, 0:1, :] += jnp.sum(dq.astype(F32), 0, keepdims=True)
        bqv_ref[0, 1:2, :] += jnp.sum(dv.astype(F32), 0, keepdims=True)
        da1_ref[rows, :] += (
            dot_nt(dq, g_ref[0, 0]) + dot_nt(dk, g_ref[0, 1]) + dot_nt(dv, g_ref[0, 2])
        )

    @pl.loop(0, D // step)
    def _(b):
        rows = pl.ds(pl.multiple_of(b * step, step), step)
        a1t = a1t_ref[rows, :]
        d0_ref[0, 0, rows, :] = dot_nn(a1t, dq_ref[...]).astype(BF16)
        d0_ref[0, 1, rows, :] = dot_nn(a1t, dk_ref[...]).astype(BF16)
        d0_ref[0, 2, rows, :] = dot_nn(a1t, dv_ref[...]).astype(BF16)
        d0_ref[0, 3, rows, :] = dot_nn(gbt_ref[rows, :], o_ref[0]).astype(BF16)

    @pl.when(t == pl.num_programs(0) - 1)
    def _():
        sums_ref[...] = jnp.zeros_like(sums_ref)

        @pl.loop(0, n // step)
        def _(b):
            rows = pl.ds(pl.multiple_of(b * step, step), step)
            xhat, r = norm_parts(x_ref[rows, :].astype(F32))
            da1 = da1_ref[rows, :]
            sums_ref[0:1, :] += jnp.sum(da1 * xhat, 0, keepdims=True)
            sums_ref[1:2, :] += jnp.sum(da1, 0, keepdims=True)
            dg = da1 * rows_ref[0:1, :]
            dv = r * (
                dg
                - jnp.mean(dg, -1, keepdims=True)
                - xhat * jnp.mean(dg * xhat, -1, keepdims=True)
            )
            xg_ref[rows, :] = (dh1_ref[rows, :] + dv).astype(BF16)


def whole(*shape):
    return pl.BlockSpec(shape, lambda t: (0,) * len(shape))


def group(*shape):
    return pl.BlockSpec((1,) + shape, lambda t: (t,) + (0,) * len(shape))


def shaped(dtype, *shape):
    return jax.ShapeDtypeStruct(shape, dtype)


SMEM_WHOLE = pl.BlockSpec(memory_space=pltpu.SMEM)


def run_attention_forward(length, x, g0, rows, bqv):
    n = x.shape[0]
    groups, _, _, width = g0.shape
    heads = width // HEAD_DIM
    return pl.pallas_call(
        attention_forward,
        grid=(groups,),
        in_specs=[SMEM_WHOLE, whole(n, D), group(4, D, width), whole(16, D), group(2, width)],
        out_specs=[
            group(n, width), group(n, width), group(width, n), group(heads, n, n),
            group(n, width), whole(D, n), whole(n, D), whole(n, D), whole(D, n),
        ],
        out_shape=[
            shaped(BF16, groups, n, width), shaped(BF16, groups, n, width),
            shaped(BF16, groups, width, n), shaped(BF16, groups, heads, n, n),
            shaped(BF16, groups, n, width), shaped(BF16, D, n), shaped(F32, n, D),
            shaped(BF16, n, D), shaped(BF16, D, n),
        ],
        scratch_shapes=[
            pltpu.VMEM((n, D), BF16), pltpu.VMEM((n, width), BF16),
            pltpu.VMEM((width, n), BF16), pltpu.VMEM((width, n), BF16),
            pltpu.VMEM((n, D), F32),
        ],
        compiler_params=pltpu.CompilerParams(vmem_limit_bytes=VMEM_LIMIT),
        name="attention_forward",
    )(length, x, g0, rows, bqv)


def run_feed_forward(length, cot, a2, a2t, h1, g1, g2, rows):
    n = cot.shape[0]
    groups, _, width = g1.shape
    return pl.pallas_call(
        feed_forward_both,
        grid=(groups,),
        in_specs=[
            SMEM_WHOLE, whole(n, D), whole(n, D), whole(D, n), whole(n, D),
            group(D, width), group(D, width), whole(16, D),
        ],
        out_specs=[
            whole(n, D), group(D, width), group(D, width), whole(n, D), whole(n, D),
            whole(D, n), whole(16, D),
        ],
        out_shape=[
            shaped(BF16, n, D), shaped(BF16, groups, D, width), shaped(BF16, groups, D, width),
            shaped(F32, n, D), shaped(BF16, n, D), shaped(BF16, D, n), shaped(F32, 16, D),
        ],
        scratch_shapes=[
            pltpu.VMEM((n, D), BF16), pltpu.VMEM((D, n), BF16), pltpu.VMEM((n, D), F32),
            pltpu.VMEM((n, D), F32), pltpu.VMEM((n, width), BF16), pltpu.VMEM((n, width), BF16),
        ],
        compiler_params=pltpu.CompilerParams(vmem_limit_bytes=VMEM_LIMIT),
        name="feed_forward_both",
    )(length, cot, a2, a2t, h1, g1, g2, rows)


def run_attention_backward(x, g0, rows, dh1, gb, gbt, q, v, kt, p, o, a1t):
    n = x.shape[0]
    groups, _, _, width = g0.shape
    heads = width // HEAD_DIM
    return pl.pallas_call(
        attention_backward,
        grid=(groups,),
        in_specs=[
            whole(n, D), group(4, D, width), whole(16, D), whole(n, D), whole(n, D),
            whole(D, n), group(n, width), group(n, width), group(width, n),
            group(heads, n, n), group(n, width), whole(D, n),
        ],
        out_specs=[group(4, D, width), whole(n, D), whole(8, D), group(8, width)],
        out_shape=[
            shaped(BF16, groups, 4, D, width), shaped(BF16, n, D), shaped(F32, 8, D),
            shaped(F32, groups, 8, width),
        ],
        scratch_shapes=[
            pltpu.VMEM((n, width), BF16), pltpu.VMEM((16, n), F32), pltpu.VMEM((width, n), F32),
            pltpu.VMEM((n, width), BF16), pltpu.VMEM((n, width), BF16),
            pltpu.VMEM((n, width), BF16), pltpu.VMEM((n, D), F32),
        ],
        compiler_params=pltpu.CompilerParams(vmem_limit_bytes=VMEM_LIMIT),
        name="attention_backward",
    )(x, g0, rows, dh1, gb, gbt, q, v, kt, p, o, a1t)


Z_DEV, Y_DEV, X_DEV, C_DEV = 4, 2, 2, 2


class Place:
    def __init__(self):
        dp, self.t = lax.axis_index("dp"), lax.axis_index("tensor")
        self.dp = dp
        self.z, self.y = dp // 2, dp % 2
        self.x, self.c = self.t // 2, self.t % 2
        self.other_y = 1 - self.y
        self.zs = [
            self.z,
            self.z + 1 - 2 * (self.z % 2),
            self.z + 2 - 4 * (self.z // 2),
            3 - self.z,
        ]
        self.ts = [
            self.t,
            self.t + 1 - 2 * (self.t % 2),
            self.t + 2 - 4 * (self.t // 2),
            3 - self.t,
        ]
        self.to_z = [dict(dp=z * 2 + self.y) for z in self.zs]
        self.to_y = dict(dp=self.z * 2 + self.other_y)
        self.to_x = dict(tensor=self.ts[2])
        self.same_t = self.to_z[1:] + [dict(dp=z * 2 + self.other_y) for z in self.zs]
        self.same_dp = [dict(tensor=t) for t in self.ts[1:]]
        self.to_core = dict(tensor=self.ts[1])

    def group(self, k):
        return lax.select(
            k == 0, self.ts[0],
            lax.select(k == 1, self.ts[1], lax.select(k == 2, self.ts[2], self.ts[3])),
        )

    def greet(self, others=None):
        barrier = pltpu.get_barrier_semaphore()
        others = others or self.to_z[1:] + [self.to_y, self.to_x, self.to_core]
        for device in others:
            pl.semaphore_signal(
                barrier, inc=1, device_id=device, device_id_type=pl.DeviceIdType.MESH
            )
        pl.semaphore_wait(barrier, len(others))


class Links:
    def __init__(self, send_sem, recv_sem):
        self.send_sem, self.recv_sem = send_sem, recv_sem
        self.copies = []

    def add(self, device, src, dst):
        number = len(self.copies)
        copy = pltpu.make_async_remote_copy(
            src_ref=src,
            dst_ref=dst,
            send_sem=self.send_sem.at[number],
            recv_sem=self.recv_sem.at[number],
            device_id=device,
            device_id_type=pl.DeviceIdType.MESH,
        )
        self.copies.append(copy)
        return copy

    def sent(self, *apart):
        for copy in self.copies:
            if all(copy is not other for other in apart):
                copy.wait_send()


def flat(copies):
    for item in copies:
        if isinstance(item, list):
            yield from flat(item)
        else:
            yield item


def start(*copies):
    for copy in flat(copies):
        copy.start()


def recv(*copies):
    for copy in flat(copies):
        copy.wait_recv()


class Gather:
    def __init__(self, links, place, own, full, order, single=True, last=True):
        every = slice(None)
        y, other = place.y, place.other_y

        def same(device, k, yy, to):
            return links.add(device, full(k, every, yy), full(to, every, yy))

        def along_z(k, yy, block):
            here, passed = full(k, place.z, yy), full(k, place.zs[2], yy)
            return [
                links.add(place.to_z[1], block, here),
                links.add(place.to_z[2], block, here),
                links.add(place.to_z[1], passed, passed),
            ]

        self.z = along_z(0, y, own)
        if order == X_Z_Y:
            self.first = [links.add(place.to_x, own, full(2, place.z, y))]
            self.far = along_z(2, y, full(2, place.z, y))
            blocks = [(0, y), (2, y), (0, other), (2, other)]
        else:
            blocks = [(0, y), (0, other), (2, y), (2, other)]
        if order == Y_Z_X:
            self.first = [links.add(place.to_y, own, full(0, place.z, y))]
            self.far = along_z(0, other, full(0, place.z, other))
        if order == Z_Y_X and single:
            self.first = [same(place.to_y, 0, y, 0)]
        if order == Z_Y_X and not single:
            self.first = [links.add(place.to_y, own, full(0, place.z, y))]
            for k in range(1, 4):
                block = full(0, place.zs[k], y)
                self.first.append(links.add(place.to_y, block, block))
        self.second = [
            same(place.to_y, k, yy, k) if order == X_Z_Y else same(place.to_x, k, yy, 2)
            for k, yy in blocks[: 2 if last else 1]
        ]
        if not last:
            blocks = [block for block in blocks if block[0] == 0]
        self.core = [same(place.to_core, k, yy, k + 1) for k, yy in blocks]


Z_Y_X, Y_Z_X, X_Z_Y = range(3)


def fused_forward(
    tie_ref, len_ref, tokens_ref, gains_ref, bias_ref, in_ref, out_ref, expand_ref,
    project_ref,
    gq_ref, gw_ref, flat1_ref, flat2_ref, rows_ref,
    q_ref, v_ref, kt_ref, p_ref, scale_ref, o_ref, a1t_out, h1_out, a2_out, a2t_out,
    own0_ref, ownw_ref, own1_ref, own2_ref, square_ref, vec_ref,
    all0_ref, allw_ref, w1_ref, w2_ref, vecs_ref, bqv_ref, x_ref, a1_ref, k_ref, qa_ref, vt_ref, ot_ref, a1t_ref, h1_ref, a2_ref, a2t_ref,
    send_sem, recv_sem, local_sem, flush_sem, row_sem,
):
    t = pl.program_id(0)
    n, _ = x_ref.shape
    width = allw_ref.shape[-1]
    heads = width // HEAD_DIM
    step = 256
    place = Place()
    length = len_ref[place.t]
    links = Links(send_sem, recv_sem)
    z, y, x, c = place.z, place.y, place.x, place.c
    mine_there = vecs_ref.at[z, y, x, c]
    column = vecs_ref.at[:, :, x, c]
    vec_one = [links.add(device, vec_ref, mine_there) for device in place.same_t]
    vec_two = [links.add(device, column, column) for device in place.same_dp]
    seg0 = Gather(
        links, place, own0_ref, lambda k, z, y: all0_ref.at[k, z, y], Z_Y_X, single=False
    )
    segw = Gather(links, place, ownw_ref, lambda k, z, y: allw_ref.at[k, z, y], Z_Y_X)
    seg1 = Gather(
        links, place, own1_ref, lambda k, z, y: w1_ref.at[k, z, y], Y_Z_X, last=False
    )
    seg2 = Gather(
        links, place, own2_ref, lambda k, z, y: w2_ref.at[k, z, y], X_Z_Y, last=False
    )
    flush = [
        [
            pltpu.make_async_copy(ref.at[k], flat.at[k], flush_sem.at[i, k])
            for k in range(3)
        ]
        for i, (ref, flat) in enumerate([(w1_ref, flat1_ref), (w2_ref, flat2_ref)])
    ]
    put_a1t = pltpu.make_async_copy(a1t_ref, a1t_out, local_sem.at[0])
    put_a2t = pltpu.make_async_copy(a2t_ref, a2t_out, local_sem.at[1])
    puts = []
    for i in range(n // step):
        rows = pl.ds(i * step, step)
        puts.append([
            pltpu.make_async_copy(h1_ref.at[rows], h1_out.at[rows], row_sem.at[0, i]),
            pltpu.make_async_copy(a2_ref.at[rows], a2_out.at[rows], row_sem.at[1, i]),
        ])
    fetch = pltpu.make_async_copy(tokens_ref.at[place.t], x_ref, local_sem.at[2])

    def relay_z(copies):
        recv(copies[1])
        start(copies[2])

    def pass_own(seg):
        recv(seg.z[0], seg.z[2])
        if seg is segw:
            start(seg.first)
        start(seg.second[0], seg.core[0])

    def pass_second(seg):
        recv(seg.second)
        if seg is seg2:
            start(seg.core[1])

    def pass_first(seg):
        recv(seg.first)
        if seg is segw:
            start(seg.second[1], seg.core[1])
        else:
            start(seg.far[1], seg.far[0])

    def pass_far(seg):
        recv(seg.far[0], seg.far[2])
        start(seg.core[1:] if seg is seg1 else [])

    def pass_core(seg, i):
        recv(seg.second[i])
        start(seg.core[2 + i])

    plan = [
        (0, 0, lambda: (pass_own(segw), pass_first(seg1), relay_z(seg2.z), pass_first(seg2))),
        (0, 3, lambda: (pass_first(segw), relay_z(seg1.z), pass_core(seg0, 0))),
        (1, 0, lambda: recv(seg0.core[:2])),
        (1, 1, lambda: relay_z(seg1.far)),
        (1, 3, lambda: pass_core(seg0, 1)),
        (1, 4, lambda: (recv(segw.core[:2]), pass_core(segw, 0), pass_own(seg2))),
        (2, 1, lambda: relay_z(seg2.far)),
        (2, 2, lambda: pass_core(segw, 1)),
        (2, 3, lambda: pass_own(seg1)),
        (3, 0, lambda: (recv(seg0.core[2:]), pass_far(seg1), flush[0][0].start())),
        (3, 2, lambda: (pass_second(seg2), flush[1][0].start())),
        (3, 3, lambda: (pass_far(seg2), flush[1][2].start())),
        (3, 4, lambda: recv(segw.core[2:])),
    ]

    def serve(point):
        for step, where, act in plan:
            if where == point:
                pl.when(t == step)(lambda act=act: (act(), None)[1])

    @pl.when(t == 0)
    def _():
        s0, s1, s2, s3 = tie_ref[0], tie_ref[1], tie_ref[2], tie_ref[3]
        fetch.start()
        square_ref[...] = jnp.zeros_like(square_ref)
        gain = gains_ref.shape[-1]
        square_ref[0:1, :gain] = gains_ref[s0].astype(F32)[0:1]
        square_ref[1:2, :gain] = gains_ref[s2].astype(F32)[1:2]
        kinds = [s0, s0, s0, s1, s2, s3, s2, s2, s2, s2]
        for i, source in enumerate(kinds):
            wide = bias_ref[i].astype(F32)
            here = lax.broadcasted_iota(jnp.int32, wide.shape, 0) == source
            square_ref[2 + i : 3 + i, :gain] = jnp.sum(
                jnp.where(here, wide, 0.0), 0, keepdims=True
            )
        vec_ref[...] = square_ref[...].T[:gain]
        for j in range(3):
            own0_ref[:, j * width : (j + 1) * width] = in_ref[s0, j]
        place.greet(place.same_t + place.same_dp)
        start(vec_one, seg0.z[1], seg0.z[0], seg0.first[0])
        vecs_ref[z, y, x, c] = vec_ref[...]
        ones = lax.broadcasted_iota(jnp.int32, (vt_ref.shape[1] - HEAD_DIM, n), 0) == 0
        for h in range(heads):
            vt_ref[h, HEAD_DIM:, :] = ones.astype(BF16)
        all0_ref[0, z, y] = own0_ref[...]
        ownw_ref[...] = out_ref[s1].T
        allw_ref[0, z, y] = ownw_ref[...]
        own1_ref[...] = expand_ref[s2]
        own2_ref[...] = project_ref[s3]
        w1_ref[0, z, y] = own1_ref[...]
        w2_ref[0, z, y] = own2_ref[...]
        recv(vec_one)
        start(vec_two)
        relay_z(seg0.z)
        start(seg0.first[2])
        recv(seg0.z[0])
        start(seg0.first[1], segw.z[1], segw.z[0], seg2.z[1])
        recv(vec_two)
        start(seg2.first)
        vecs = vecs_ref[...].reshape(D, vecs_ref.shape[-1]).T[:16]
        rows_ref[...] = vecs
        recv(seg0.z[2])
        start(seg0.first[3], seg1.first, seg0.second[0], seg0.core[0])
        for k in range(4):
            part = slice(k * width, (k + 1) * width)
            bqv_ref[k, 0:1, :width] = vecs[3:4, part]
            bqv_ref[k, 0:1, width : 2 * width] = jnp.zeros((1, width), F32)
            bqv_ref[k, 0:1, 2 * width :] = vecs[4:5, part]
        fetch.wait()

        @pl.loop(0, n // step)
        def _(b):
            rows = pl.ds(pl.multiple_of(b * step, step), step)
            wide = x_ref[rows, :].astype(F32)
            xhat, _ = norm_parts(wide)
            a1 = (xhat * rows_ref[0:1, :] + rows_ref[2:3, :]).astype(BF16)
            a1_ref[rows, :] = a1
            a1t_ref[:, rows] = a1.T
            h1_ref[rows, :] = wide + rows_ref[5:6, :]

        put_a1t.start()
        relay_z(segw.z)
        start(seg2.z[0], seg1.z[1], seg1.z[0])
        recv(seg0.first)
        start(seg0.second[1], seg0.core[1])

    serve(0)
    gq = all0_ref[t].reshape(D, 3 * width)
    gq_ref[0] = gq
    mine = place.group(t)
    qkv = dot_nn(a1_ref[...], gq) + bqv_ref[mine, 0:1, :]
    q = qkv[:, :width].astype(BF16) * jnp.asarray(HEAD_DIM ** -0.5, BF16)
    k = qkv[:, width : 2 * width].astype(BF16)
    v = qkv[:, 2 * width :].astype(BF16)
    q_ref[0] = q
    kt_ref[0] = k.T
    v_ref[0] = v
    vt = v.T
    for h in range(heads):
        vt_ref[h, :HEAD_DIM, :] = vt[h * HEAD_DIM : (h + 1) * HEAD_DIM]
    spare = k_ref.shape[1] - width
    dead = lax.broadcasted_iota(jnp.int32, (n, spare), 0) >= length
    first_column = lax.broadcasted_iota(jnp.int32, (n, spare), 1) == 0
    k_ref[:, :width] = k
    k_ref[:, width:] = jnp.where(first_column & dead, MASKED, 0.0).astype(BF16)
    qa_ref[:, :width] = q
    qa_ref[:, width:] = jnp.where(first_column, 1.0, 0.0).astype(BF16)

    serve(1)
    def scores(h, b):
        first, last = b * step, (b + 1) * step
        q = qa_ref[first:last, :]
        lane = lax.broadcasted_iota(jnp.int32, (1, q.shape[1]), 1)
        keep = head_mask((1, q.shape[1]), h) | (lane >= width)
        return dot_nt(k_ref[:last, :], jnp.where(keep, q, jnp.zeros((), BF16)))

    def attend(h, b, s):
        first, last = b * step, (b + 1) * step
        key = lax.broadcasted_iota(jnp.int32, (step, step), 0)
        query = lax.broadcasted_iota(jnp.int32, (step, step), 1)
        near = jnp.where(key <= query, s[first:], MASKED)
        top = jnp.max(near, 0, keepdims=True)
        if b:
            far = s[:first]
            top = jnp.maximum(top, jnp.max(far, 0, keepdims=True))
        e_near = jnp.exp((near - top).astype(BF16))
        p_ref[0, h, first:last, first:last] = e_near
        o = dot_nn(vt_ref[h, :, first:last], e_near)
        if b:
            e_far = jnp.exp((far - top).astype(BF16))
            p_ref[0, h, :first, first:last] = e_far
            o += dot_nn(vt_ref[h, :, :first], e_far)
        scale = 1.0 / o[HEAD_DIM : HEAD_DIM + 1]
        scale_ref[0, h : h + 1, first:last] = scale
        ot_ref[h * HEAD_DIM : (h + 1) * HEAD_DIM, first:last] = (
            o[:HEAD_DIM] * scale
        ).astype(BF16)

    scale_ref[0, heads:, :] = jnp.zeros((scale_ref.shape[1] - heads, n), F32)
    for h in range(heads):
        s = scores(h, 0)
        for b in range(n // step):
            ahead = scores(h, b + 1) if b + 1 < n // step else None
            attend(h, b, s)
            s = ahead
        serve(2 + h)

    gw_ref[0] = allw_ref[t].reshape(gw_ref.shape[1:])
    o = ot_ref[...].T
    o_ref[0] = o
    h1_ref[...] += dot_nt(o, gw_ref[0])

    @pl.when(t == 3)
    def _():
        for i, rows in enumerate(blocks(n, step)):
            xhat, _ = norm_parts(h1_ref[rows, :])
            a2 = (xhat * rows_ref[1:2, :] + rows_ref[6:7, :]).astype(BF16)
            a2_ref[rows, :] = a2
            a2t_ref[:, rows] = a2.T
            for put in puts[i]:
                put.start()
        put_a2t.start()
        recv(seg2.core)
        flush[1][1].start()
        recv(seg1.core)
        flush[0][1].start()
        pass_second(seg1)
        flush[0][2].start()
        links.sent()
        for copies in flush + puts + [[put_a1t, put_a2t]]:
            for copy in copies:
                copy.wait()


N_GATHER = 10 + 13 + 10 + 10 + 10
VMEM_WHOLE = pl.BlockSpec(memory_space=pltpu.VMEM)
ANY_WHOLE = pl.BlockSpec(memory_space=pl.ANY)


def run_fused_forward(tie, lengths, tokens, gains, biases, w_in, w_out, w_expand, w_project):
    groups, n, _ = tokens.shape
    depth, width = w_in.shape[-2:]
    heads = width // HEAD_DIM
    hidden = w_expand.shape[-1]
    w_project = w_project.transpose(0, 2, 1)
    biases = biases.transpose(1, 0, 2)
    own = gains.shape[-1]
    return pl.pallas_call(
        fused_forward,
        grid=(groups,),
        in_specs=[SMEM_WHOLE, SMEM_WHOLE, ANY_WHOLE] + [VMEM_WHOLE] * 6,
        out_specs=[
            group(D, 3 * width), group(D, width), ANY_WHOLE, ANY_WHOLE, VMEM_WHOLE,
            group(n, width), group(n, width), group(width, n), group(heads, n, n),
            group(8, n), group(n, width), ANY_WHOLE, ANY_WHOLE, ANY_WHOLE, ANY_WHOLE,
        ],
        out_shape=[
            shaped(BF16, groups, D, 3 * width), shaped(BF16, groups, D, width),
            shaped(BF16, groups, Z_DEV, Y_DEV, depth, hidden),
            shaped(BF16, groups, Z_DEV, Y_DEV, depth, hidden),
            shaped(F32, 16, D),
            shaped(BF16, groups, n, width), shaped(BF16, groups, n, width),
            shaped(BF16, groups, width, n), shaped(BF16, groups, heads, n, n),
            shaped(F32, groups, 8, n), shaped(BF16, groups, n, width), shaped(BF16, D, n), shaped(F32, n, D),
            shaped(BF16, n, D), shaped(BF16, D, n),
        ],
        scratch_shapes=[
            pltpu.VMEM((depth, 3 * width), BF16), pltpu.VMEM((depth, width), BF16),
            pltpu.VMEM((depth, hidden), BF16), pltpu.VMEM((depth, hidden), BF16),
            pltpu.VMEM((128, 128), F32), pltpu.VMEM((own, 128), F32),
            pltpu.VMEM((groups, Z_DEV, Y_DEV, depth, 3 * width), BF16),
            pltpu.VMEM((groups, Z_DEV, Y_DEV, depth, width), BF16),
            pltpu.VMEM((groups, Z_DEV, Y_DEV, depth, hidden), BF16),
            pltpu.VMEM((groups, Z_DEV, Y_DEV, depth, hidden), BF16),
            pltpu.VMEM((Z_DEV, Y_DEV, X_DEV, C_DEV, own, 128), F32),
            pltpu.VMEM((groups, 8, 3 * width), F32),
            pltpu.VMEM((n, D), BF16), pltpu.VMEM((n, D), BF16), pltpu.VMEM((n, 256), BF16),
            pltpu.VMEM((n, 256), BF16), pltpu.VMEM((heads, HEAD_DIM + 16, n), BF16),
            pltpu.VMEM((width, n), BF16),
            pltpu.VMEM((D, n), BF16), pltpu.VMEM((n, D), F32), pltpu.VMEM((n, D), BF16),
            pltpu.VMEM((D, n), BF16),
            pltpu.SemaphoreType.DMA((N_GATHER,)), pltpu.SemaphoreType.DMA((N_GATHER,)),
            pltpu.SemaphoreType.DMA((3,)), pltpu.SemaphoreType.DMA((2, 4)),
            pltpu.SemaphoreType.DMA((2, n // 256)),
        ],
        compiler_params=pltpu.CompilerParams(
            vmem_limit_bytes=VMEM_LIMIT, collective_id=0, has_side_effects=True
        ),
        name="fused_forward",
    )(tie, lengths, tokens, gains, biases, w_in, w_out, w_expand, w_project)


class Result:
    def __init__(self, links, place, own_ref, passing_ref, out_ref, step, sem):
        count = own_ref.shape[0] // step
        self.x, self.core, self.far, self.keep, self.keep_far = [], [], [], [], []
        for i in range(count):
            rows = pl.ds(i * step, step)
            mine, theirs = out_ref.at[place.t, rows], out_ref.at[place.ts[2], rows]
            own, passing = own_ref.at[rows], passing_ref.at[rows]
            self.x.append(links.add(place.to_x, own, passing))
            self.core.append(links.add(place.to_core, own, mine))
            self.far.append(links.add(place.to_core, passing, theirs))
            self.keep.append(pltpu.make_async_copy(own, mine, sem.at[0, i]))
            self.keep_far.append(pltpu.make_async_copy(passing, theirs, sem.at[1, i]))

    def send(self, i):
        start(self.x[i], self.core[i], self.keep[i])

    def pass_on(self, i):
        recv(self.x[i])
        start(self.far[i], self.keep_far[i])

    def finish(self):
        recv(self.core, self.far)
        for copy in self.keep + self.keep_far:
            copy.wait()


def low(value):
    return jnp.asarray(value, BF16)


def pair_order(i):
    return i + 1 - 2 * (i % 2)


def fused_feed_forward(
    len_ref, cot_ref, a2_ref, a2t_in, h1_in, far1_ref, far2_ref, rows_ref,
    out_out, fold_ref, work_out, dh1_out, gb_out, gbt_out, sums_ref,
    gf_ref, gft_ref, feed_ref, da2_ref, h_ref, df_ref, weights_ref, missing_ref, third_ref,
    stage_ref, land_ref, near_ref, cross_ref, a2t_ref, h1_ref, out_ref, work_ref,
    send_sem, recv_sem, local_sem, row_sem,
):
    t = pl.program_id(0)
    n = gf_ref.shape[0]
    step = 256
    depth = stage_ref.shape[-2]
    place = Place()
    length = len_ref[place.t]
    links = Links(send_sem, recv_sem)
    y, other = place.y, place.other_y
    last = [
        links.add(place.to_x, far1_ref.at[0, :, other], missing_ref.at[0, 0]),
        links.add(place.to_y, far2_ref.at[2, :, y], missing_ref.at[1, 0]),
    ]
    last_core = [
        links.add(place.to_core, missing_ref.at[i, 0], missing_ref.at[i, 1]) for i in range(2)
    ]
    third = [
        links.add(place.to_core, far_ref.at[2, :, y], third_ref.at[i])
        for i, far_ref in enumerate([far1_ref, far2_ref])
    ]
    core = [
        [links.add(place.to_core, stage_ref.at[i], land_ref.at[s, i]) for i in range(2)]
        for s in range(2)
    ]
    cross = [
        links.add(place.to_y, near_ref.at[i, :, other], cross_ref.at[i]) for i in range(2)
    ]
    fetch = pltpu.make_async_copy(cot_ref.at[place.t], gf_ref, local_sem.at[0])
    gb_ref, gbt_ref, dh1_ref = gf_ref, gft_ref, da2_ref
    late = [
        pltpu.make_async_copy(a2t_in, a2t_ref, local_sem.at[5]),
        pltpu.make_async_copy(h1_in, h1_ref, local_sem.at[6]),
    ]
    puts = []
    for i in range(n // step):
        rows = pl.ds(i * step, step)
        puts.append([
            pltpu.make_async_copy(ref.at[rows], out.at[rows], row_sem.at[j, i])
            for j, (ref, out) in enumerate(
                [(out_ref, out_out), (dh1_ref, dh1_out), (gb_ref, gb_out)]
            )
        ])
    put_gbt = pltpu.make_async_copy(gbt_ref, gbt_out, local_sem.at[7])
    put_work = pltpu.make_async_copy(work_ref, work_out, local_sem.at[8])
    k = pair_order(t)
    mine = place.group(k)

    def load(step, whole, slot):
        for i, far_ref in enumerate([far1_ref, far2_ref]):
            group = far_ref.at[pair_order(step)]
            to = weights_ref.at[slot, i]
            if not whole:
                group, to = group.at[:, y], to.at[:, y]
            yield pltpu.make_async_copy(group, to, local_sem.at[1 + 2 * slot + i])

    def live_rows(b):
        at = b * step + lax.broadcasted_iota(jnp.int32, (step, 1), 0)
        return (at < length).astype(F32)

    @pl.when(t == 0)
    def _():
        fetch.start()
        for copy in load(0, True, 0):
            copy.start()
        for copy in late:
            copy.start()
        place.greet()
        start(last, third)
        sums_ref[...] = jnp.zeros_like(sums_ref)
        feed_ref[...] = jnp.zeros_like(feed_ref)
        da2_ref[...] = jnp.zeros_like(da2_ref)
        fetch.wait()

        @pl.loop(0, n // step)
        def _(b):
            rows = pl.ds(pl.multiple_of(b * step, step), step)
            g = (gf_ref[rows, :].astype(F32) * live_rows(b)).astype(BF16)
            gf_ref[rows, :] = g
            gft_ref[:, rows] = g.T
            sums_ref[7:8, :] += jnp.sum(g.astype(F32), 0, keepdims=True)

    for i in range(4):
        @pl.when(t == i)
        def _():
            if i == 2:
                recv(last_core, third)
            else:
                for copy in load(i, i < 2, i % 2):
                    copy.wait()
            if i in (0, 2):
                for copy in load(i + 1, i + 1 < 2, (i + 1) % 2):
                    copy.start()
            for j in range(2):
                if i == 2:
                    weights_ref[0, j, :, y] = third_ref[j]
                if i >= 2:
                    weights_ref[i % 2, j, :, other] = missing_ref[j, 3 - i]

    bias = rows_ref[pl.ds(8 + mine, 1), :]
    w1 = weights_ref[t % 2, 0].reshape(D, -1)
    w2 = weights_ref[t % 2, 1].reshape(D, -1)
    column = jnp.zeros((1, w1.shape[1]), F32)
    for rows in blocks(n, step):
        f = (dot_nn(a2_ref[rows, :], w1) + bias).astype(BF16)
        dh = dot_nn(gf_ref[rows, :], w2)
        f2 = f * f
        th = jnp.tanh(f * (low(SQRT_2_PI) + low(SQRT_2_PI * 0.044715) * f2))
        half = low(0.5) + low(0.5) * th
        h = f * half
        slope = half + f * (low(0.5) - low(0.5) * th * th) * (
            low(SQRT_2_PI) + low(3 * SQRT_2_PI * 0.044715) * f2
        )
        df = (dh * slope.astype(F32)).astype(BF16)
        h_ref[rows, :] = h
        df_ref[rows, :] = df
        column += jnp.sum(df.astype(F32), 0, keepdims=True)
        feed_ref[rows, :] += dot_nt(h, w2)
        da2_ref[rows, :] += dot_nt(df, w1)
    sums_ref[pl.ds(8 + mine, 1), :] = column

    @pl.when(t == 1)
    def _():
        recv(last)
        start(last_core)

    @pl.when(t == 0)
    def _():
        late[0].wait()

    def weight_grad(left_ref, right_ref):
        value = dot_nn(left_ref[...], right_ref[...])
        return value.reshape(Z_DEV, Y_DEV, depth, value.shape[-1]).astype(BF16)

    grad1 = weight_grad(a2t_ref, df_ref)
    grad2 = weight_grad(gft_ref, h_ref)

    def put(ref):
        ref[0] = grad1
        ref[1] = grad2

    def reduced(ref):
        return lambda i, s, z: (
            ref[i, z].astype(F32) + land_ref[s, i, z].astype(F32)
        ).astype(BF16)

    @pl.when(t == 0)
    def _():
        put(stage_ref)
        start(core[0])

    @pl.when(t == 1)
    def _():
        put(near_ref)
        recv(core[0])

        @pl.loop(0, Z_DEV)
        def _(z):
            for i in range(2):
                near_ref[i, z] = reduced(near_ref)(i, 0, z)

        start(cross)

    @pl.when(t == 2)
    def _():
        for copy in core[0]:
            copy.wait_send()
        put(stage_ref)
        start(core[1])

    @pl.when(t == 3)
    def _():
        put(work_ref)
        late[1].wait()
        for i, rows in enumerate(blocks(n, step)):
            live = live_rows(i)
            h1 = h1_ref[rows, :]
            out_ref[rows, :] = (live * (h1 + (feed_ref[rows, :] + rows_ref[7:8, :]))).astype(BF16)
            xhat, r = norm_parts(h1)
            da2 = da2_ref[rows, :]
            sums_ref[1:2, :] += jnp.sum(da2 * xhat, 0, keepdims=True)
            sums_ref[6:7, :] += jnp.sum(da2, 0, keepdims=True)
            dg = da2 * rows_ref[1:2, :]
            dv = r * (
                dg
                - jnp.mean(dg, -1, keepdims=True)
                - xhat * jnp.mean(dg * xhat, -1, keepdims=True)
            )
            dh1 = gf_ref[rows, :].astype(F32) + dv
            dh1_ref[rows, :] = dh1
            gb = dh1.astype(BF16)
            gb_ref[rows, :] = gb
            gbt_ref[:, rows] = gb.T
            sums_ref[5:6, :] += jnp.sum(gb.astype(F32), 0, keepdims=True)
            for copy in puts[i]:
                copy.start()
        put_gbt.start()
        recv(core[1])

        @pl.loop(0, Z_DEV)
        def _(z):
            for i in range(2):
                work_ref[i, z] = reduced(work_ref)(i, 1, z)

        put_work.start()
        recv(cross)

        @pl.loop(0, Z_DEV)
        def _(z):
            for i in range(2):
                fold_ref[i, z] = (
                    near_ref[i, z, y].astype(F32) + cross_ref[i, z].astype(F32)
                ).astype(BF16)

        links.sent(*core[0])
        for copies in puts + [[put_gbt, put_work]]:
            for copy in copies:
                copy.wait()


def run_fused_feed_forward(lengths, cot, a2, a2t, h1, g1, g2, rows):
    n = cot.shape[1]
    groups, _, _, depth, hidden = g1.shape
    both = (2, Z_DEV, Y_DEV, depth, hidden)
    fold = (2, Z_DEV, depth, hidden)
    return pl.pallas_call(
        fused_feed_forward,
        grid=(groups,),
        in_specs=[SMEM_WHOLE, ANY_WHOLE, VMEM_WHOLE] + [ANY_WHOLE] * 4 + [VMEM_WHOLE],
        out_specs=[ANY_WHOLE, VMEM_WHOLE] + [ANY_WHOLE] * 4 + [VMEM_WHOLE],
        out_shape=[
            shaped(BF16, n, D), shaped(BF16, *fold), shaped(BF16, *both), shaped(F32, n, D),
            shaped(BF16, n, D), shaped(BF16, D, n), shaped(F32, 16, D),
        ],
        scratch_shapes=[
            pltpu.VMEM((n, D), BF16), pltpu.VMEM((D, n), BF16), pltpu.VMEM((n, D), F32),
            pltpu.VMEM((n, D), F32), pltpu.VMEM((n, hidden), BF16), pltpu.VMEM((n, hidden), BF16),
            pltpu.VMEM((2,) + both, BF16),
            pltpu.VMEM((2,) + fold, BF16), pltpu.VMEM(fold, BF16), pltpu.VMEM(both, BF16),
            pltpu.VMEM((2,) + both, BF16),
            pltpu.VMEM(both, BF16), pltpu.VMEM(fold, BF16),
            pltpu.VMEM((D, n), BF16), pltpu.VMEM((n, D), F32), pltpu.VMEM((n, D), BF16),
            pltpu.VMEM(both, BF16),
            pltpu.SemaphoreType.DMA((12,)), pltpu.SemaphoreType.DMA((12,)),
            pltpu.SemaphoreType.DMA((9,)), pltpu.SemaphoreType.DMA((3, n // 256)),
        ],
        compiler_params=pltpu.CompilerParams(
            vmem_limit_bytes=VMEM_LIMIT, collective_id=1, has_side_effects=True
        ),
        name="fused_feed_forward",
    )(lengths, cot, a2, a2t, h1, g1, g2, rows)
class Reduce:
    def __init__(
        self, links, place, work, acc, cross_ref, far_ref, mid_ref, last_ref, side_ref,
        slots=(0, 1),
    ):
        self.place, self.work, self.acc = place, work, acc
        self.cross_ref, self.far_ref, self.mid_ref = cross_ref, far_ref, mid_ref
        self.last_ref, self.side_ref = last_ref, side_ref
        zs = place.zs
        self.y = {
            s: [
                links.add(place.to_y, work(s, zs[j], place.other_y), cross_ref.at[s, zs[j]])
                for j in (1, 3, 2, 0)
            ]
            for s in slots
        }
        self.z = [
            [
                links.add(place.to_z[1], acc(s, zs[1]), far_ref.at[s, 0]),
                links.add(place.to_z[1], acc(s, zs[3]), far_ref.at[s, 1]),
                links.add(place.to_z[2], mid_ref.at[s, 1], far_ref.at[s, 2]),
            ]
            for s in range(2)
        ]
        self.x = links.add(place.to_x, last_ref, side_ref)

    def fold_y(self, s, half):
        for i, j in [(0, 1), (1, 3), (2, 2), (3, 0)][2 * half : 2 * half + 2]:
            z = self.place.zs[j]
            recv(self.y[s][i])
            value = self.work(s, z, self.place.y)[...].astype(F32)
            self.acc(s, z)[...] = (value + self.cross_ref[s, z].astype(F32)).astype(BF16)
            if i < 2:
                start(self.z[s][i])

    def fold_z(self, s):
        recv(self.z[s][:2])
        for i in (1, 0):
            value = self.acc(s, self.place.zs[2 * i])[...].astype(F32)
            self.mid_ref[s, i] = (value + self.far_ref[s, i].astype(F32)).astype(BF16)
            if i:
                start(self.z[s][2])

    def own(self, s):
        recv(self.z[s][2])
        return self.mid_ref[s, 0].astype(F32) + self.far_ref[s, 2].astype(F32)

    def send_x(self):
        self.last_ref[...] = self.own(1).astype(BF16)
        start(self.x)

    def total(self):
        value = self.own(0)
        recv(self.x)
        return value + self.side_ref[...].astype(F32)


def fused_backward(
    tokens_ref, gq_in, gw_in, rows_ref, dh1_ref, gb_ref, gbt_in, q_in, v_in, kt_in,
    p_ref, scale_in, o_in, a1t_in, layer_in, fold_in, work_in, early_ref,
    out_ref, layerout_ref, part0_ref, partw_ref, part1_ref, part2_ref, total_ref,
    gq_ref, gw_ref, q_ref, v_ref, kt_ref, scale_ref, o_ref,
    a1t_ref, gbt_ref, layer_ref, fold_ref, work_ref, do_ref, delta_ref, dkv_ref, dqkv_ref, da1_ref, own_ref, passing_ref, passlayer_ref, bqv_ref,
    folded_ref, cross1_ref, far1_ref, mid1_ref, last1_ref, side1_ref,
    cross2_ref, far2_ref, mid2_ref, last2_ref, side2_ref,
    stagew_ref, landw_ref, workw_ref, crossw_ref, farw_ref, midw_ref, lastw_ref, sidew_ref,
    stage0_ref, land0_ref, work0_ref, cross0_ref, far0_ref, mid0_ref, last0_ref, side0_ref,
    sums_ref, sumland_ref,
    send_sem, recv_sem, local_sem, result_sem, group_sem,
):
    t = pl.program_id(0)
    n = own_ref.shape[0]
    width = gw_ref.shape[-1]
    depth = part0_ref.shape[0]
    heads = width // HEAD_DIM
    step = n // 4
    place = Place()
    y = place.y
    links = Links(send_sem, recv_sem)
    k, i = group_and_block(t)
    mine = place.group(k)
    now = k % 2
    out = Result(links, place, own_ref, passing_ref, out_ref, step, result_sem.at[0])
    layer = Result(links, place, layer_ref, passlayer_ref, layerout_ref, step, result_sem.at[1])
    fetch = pltpu.make_async_copy(tokens_ref.at[place.t], own_ref, local_sem.at[0])
    fetch_layer, fetch_work, fetch_fold, fetch_gbt, fetch_a1t = [
        pltpu.make_async_copy(there, here, local_sem.at[1 + j])
        for j, (there, here) in enumerate([
            (layer_in, layer_ref), (work_in, work_ref), (fold_in, fold_ref),
            (gbt_in, gbt_ref), (a1t_in, a1t_ref),
        ])
    ]
    def operands(group):
        slot = group % 2
        pairs = [
            (gw_in, gw_ref), (scale_in, scale_ref), (o_in, o_ref), (v_in, v_ref),
            (q_in, q_ref), (kt_in, kt_ref), (gq_in, gq_ref),
        ]
        return [
            pltpu.make_async_copy(there.at[group], here.at[slot], group_sem.at[slot, j])
            for j, (there, here) in enumerate(pairs)
        ]

    corew = [links.add(place.to_core, stagew_ref, landw_ref.at[i]) for i in range(2)]
    core0 = [links.add(place.to_core, stage0_ref, land0_ref.at[i]) for i in range(2)]
    def half_done(i, *landing):
        return Reduce(
            links, place, lambda s, z, y: work_ref.at[i, z, y],
            lambda s, z: folded_ref.at[i, z] if s else fold_ref.at[i, z],
            *landing, slots=(1,),
        )

    seg1 = half_done(0, cross1_ref, far1_ref, mid1_ref, last1_ref, side1_ref)
    seg2 = half_done(1, cross2_ref, far2_ref, mid2_ref, last2_ref, side2_ref)
    segw = Reduce(
        links, place, lambda s, z, y: workw_ref.at[s, z, y],
        lambda s, z: workw_ref.at[s, z, y],
        crossw_ref, farw_ref, midw_ref, lastw_ref, sidew_ref,
    )
    seg0 = Reduce(
        links, place, lambda s, z, y: work0_ref.at[s, z, y],
        lambda s, z: work0_ref.at[s, z, y],
        cross0_ref, far0_ref, mid0_ref, last0_ref, side0_ref,
    )
    sum_core, sum_y, *sum_z, sum_x = [
        links.add(to, sums_ref.at[i], sumland_ref.at[j])
        for j, (i, to) in enumerate(
            zip([0, 1, 2, 2, 2, 3], [place.to_core, place.to_y] + place.to_z[1:] + [place.to_x])
        )
    ]

    def when(point):
        return pl.when(t == point)

    @when(0)
    def _():
        start(fetch_layer, operands(1), fetch_work, fetch_fold, fetch_gbt, operands(0))
        start(fetch, fetch_a1t)
        place.greet()
        fetch_layer.wait()
        for i in range(4):
            layer.send(i)
        fetch_work.wait()
        start(seg1.y[1], seg2.y[1])
        fetch_fold.wait()
        start(seg1.z[0][:2], seg2.z[0][:2])
        bqv_ref[...] = jnp.zeros_like(bqv_ref)
        sums_ref[0] = early_ref[...]
        da1_ref[...] = jnp.zeros_like(da1_ref)
        fetch_gbt.wait()

    def add_core():
        recv(corew[1])

        @pl.loop(0, Z_DEV)
        def _(z):
            workw_ref[1, z] = (
                workw_ref[1, z].astype(F32) + landw_ref[1, z].astype(F32)
            ).astype(BF16)

        start(segw.y[1])

    def wait(copies):
        for copy in copies:
            copy.wait()

    @when(0)
    def _():
        wait(operands(1))

    @when(4)
    def _():
        start(operands(3))
        wait(operands(0))

    @when(8)
    def _():
        start(operands(2))
        wait(operands(3))

    @when(9)
    def _():
        wait(operands(2))

    plan = [
        (2, 1, lambda: (seg1.fold_y(1, 0), seg1.fold_z(0))),
        (3, 1, lambda: layer.pass_on(0)),
        (4, 0, lambda: (seg1.fold_y(1, 1), seg2.fold_z(0))),
        (4, 1, lambda: layer.pass_on(1)),
        (5, 1, lambda: (seg1.fold_z(1), seg2.fold_y(1, 0))),
        (8, 0, lambda: (seg2.fold_y(1, 1), layer.pass_on(2))),
        (8, 1, lambda: (seg1.send_x(), segw.fold_y(0, 0), segw.fold_y(0, 1))),
        (9, 0, add_core),
        (9, 1, lambda: (seg2.fold_z(1), seg0.fold_y(0, 0), layer.pass_on(3))),
        (10, 1, lambda: segw.fold_z(0)),
        (11, 1, lambda: (seg2.send_x(), seg0.fold_y(0, 1))),
        (12, 1, lambda: (segw.fold_y(1, 0), segw.fold_y(1, 1))),
        (13, 1, lambda: (seg0.fold_z(0), out.pass_on(3))),
        (14, 1, lambda: segw.fold_z(1)),
    ]

    def serve(point):
        for at, where, act in plan:
            if where == point:
                pl.when(t == at)(lambda act=act: (act(), None)[1])

    @pl.when((t == 0) | (t == 4) | (t == 8) | (t == 9))
    def _():
        pick = (
            lax.broadcasted_iota(jnp.int32, (8, width), 1) // HEAD_DIM
            == lax.broadcasted_iota(jnp.int32, (8, width), 0)
        ).astype(BF16)

        @pl.loop(0, n // step)
        def _(i):
            rows = pl.ds(pl.multiple_of(i * step, step), step)
            columns = scale_ref[now, :, rows].T
            lane = lax.broadcasted_iota(jnp.int32, (step, width), 1)
            scale = columns[:, heads - 1 : heads]
            for h in reversed(range(heads - 1)):
                scale = jnp.where(lane < (h + 1) * HEAD_DIM, columns[:, h : h + 1], scale)
            do = (dot_nn(gb_ref[rows, :], gw_ref[now]) * scale).astype(BF16)
            do_ref[now, rows, :] = do
            product = do.astype(F32) * o_ref[now, rows, :].astype(F32)
            high = product.astype(BF16)
            low = (product - high.astype(F32)).astype(BF16)
            delta_ref[now, :, rows] = dot_nt(pick, high) + dot_nt(pick, low)

        value = dot_nn(gbt_ref[...], o_ref[now]).reshape(Z_DEV, Y_DEV, depth, width)
        for s in range(2):
            @when(8 * s)
            def _():
                if s:
                    corew[0].wait_send()
                stagew_ref[...] = value.astype(BF16)
                start(corew[s])

        @when(4)
        def _():
            recv(corew[0])
            workw_ref[0] = (value + landw_ref[0].astype(F32)).astype(BF16)
            start(segw.y[0])

        @when(9)
        def _():
            workw_ref[1] = value.astype(BF16)

    serve(0)

    for ii in reversed(range(4)):
        @pl.when(i == ii)
        def _():
            first, last = ii * step, (ii + 1) * step
            do = do_ref[now, first:last, :]
            q = q_ref[now, first:last, :]
            v = v_ref[now, :last, :]
            lane = lax.broadcasted_iota(jnp.int32, (1, width), 1)
            dk, dv, dq = None, None, []
            for h in range(heads):
                low, high = h * HEAD_DIM, (h + 1) * HEAD_DIM
                here = (lane >= low) & (lane < high)
                p = p_ref[0, h, :last, :]
                dp = dot_nt(v, jnp.where(here, do, jnp.zeros((), BF16)))
                ds = p * (dp - delta_ref[now, h : h + 1, first:last]).astype(BF16)
                part = dot_nn(p, do)
                dv = part if dv is None else jnp.where(lane < low, dv, part)
                part = dot_nn(ds, q)
                dk = part if dk is None else jnp.where(lane < low, dk, part)
                dq.append(dot_nn(kt_ref[now, low:high, :last], ds))
            if ii == 3:
                dkv_ref[now, 0] = dk
                dkv_ref[now, 1] = dv
            else:
                dkv_ref[now, 0, :last, :] += dk
                dkv_ref[now, 1, :last, :] += dv
            dk = dkv_ref[now, 0, first:last, :].astype(BF16)
            dv = dkv_ref[now, 1, first:last, :].astype(BF16)
            dq = (jnp.concatenate(dq, 0) * HEAD_DIM ** -0.5).astype(BF16).T
            dqkv_ref[now, first:last, :width] = dq
            dqkv_ref[now, first:last, width : 2 * width] = dk
            dqkv_ref[now, first:last, 2 * width :] = dv
            bqv_ref[mine, 0:1, :] += jnp.sum(dq.astype(F32), 0, keepdims=True)
            bqv_ref[mine, 1:2, :] += jnp.sum(dv.astype(F32), 0, keepdims=True)
            da1_ref[first:last, :] += dot_nt(dqkv_ref[now, first:last, :], gq_ref[now])

    serve(1)

    @pl.when((t > 8) & (t % 2 == 1))
    def _():
        rows = pl.ds(pl.multiple_of(i * step, step), step)
        xhat, r = norm_parts(own_ref[rows, :].astype(F32))
        da1 = da1_ref[rows, :]
        sums_ref[0, 0:1, :] += jnp.sum(da1 * xhat, 0, keepdims=True)
        sums_ref[0, 2:3, :] += jnp.sum(da1, 0, keepdims=True)
        dg = da1 * rows_ref[0:1, :]
        dv = r * (
            dg
            - jnp.mean(dg, -1, keepdims=True)
            - xhat * jnp.mean(dg * xhat, -1, keepdims=True)
        )
        own_ref[rows, :] = (dh1_ref[...] + dv).astype(BF16)
        for ii in range(4):
            @pl.when(i == ii)
            def _():
                out.send(ii)

    @pl.when((t == 3) | (t == 7) | (t > 13))
    def _():
        @when(3)
        def _():
            fetch.wait()
            fetch_a1t.wait()

        value = dot_nn(a1t_ref[...], dqkv_ref[now]).reshape(Z_DEV, Y_DEV, depth, 3 * width)
        for s in range(2):
            @when(3 + 11 * s)
            def _():
                if s:
                    core0[0].wait_send()
                stage0_ref[...] = value.astype(BF16)
                start(core0[s])

            @when(7 + 8 * s)
            def _():
                recv(core0[s])
                work0_ref[s] = (value + land0_ref[s].astype(F32)).astype(BF16)
                start(seg0.y[s])

    @when(15)
    def _():
        for s in range(4):
            sums_ref[0, 3:5, s * width : (s + 1) * width] = bqv_ref[s, 0:2, :]
        start(sum_core)
        segw.send_x()
        out.pass_on(2)
        recv(sum_core)
        sums_ref[1] = sums_ref[0] + sumland_ref[0]
        start(sum_y)
        seg0.fold_y(1, 0)
        out.pass_on(1)
        seg0.fold_y(1, 1)
        recv(sum_y)
        sums_ref[2] = sums_ref[1] + sumland_ref[1]
        start(sum_z)
        seg0.fold_z(1)
        recv(sum_z)
        sums_ref[3] = (sums_ref[2] + sumland_ref[2]) + (sumland_ref[3] + sumland_ref[4])
        start(sum_x)
        part1_ref[...] = seg1.total()
        part2_ref[...] = seg2.total()
        seg0.send_x()
        partw_ref[...] = segw.total()
        layer.finish()
        out.pass_on(0)
        recv(sum_x)
        total_ref[...] = sums_ref[3] + sumland_ref[5]
        part0_ref[...] = seg0.total()
        out.finish()
        links.sent(corew[0], core0[0])


def group_and_block(t):
    early = t < 8
    return (
        jnp.where(early, 1 - t // 4, 3 - t % 2),
        3 - jnp.where(early, t % 4, jnp.maximum(t - 8, 0) // 2),
    )


def run_fused_backward(
    tokens, gq, gw, rows, dh1, gb, gbt, q, v, kt, p, scale, o, a1t, layer, fold, work, early
):
    groups, n, _ = tokens.shape
    width = gw.shape[-1]
    heads = width // HEAD_DIM
    hidden = fold.shape[-1]
    depth = D // (Z_DEV * Y_DEV)
    step = n // 4

    p_spec = pl.BlockSpec(
        (1, heads, n, step),
        lambda t: (group_and_block(t)[0], 0, 0, group_and_block(t)[1]),
    )

    copies = 2 * 12 + 4 + 2 * 15 + 2 * 11 + 6

    def landing(lanes):
        return [
            pltpu.VMEM((2, Z_DEV, depth, lanes), BF16),
            pltpu.VMEM((2, 3, depth, lanes), BF16), pltpu.VMEM((2, 2, depth, lanes), BF16),
            pltpu.VMEM((depth, lanes), BF16), pltpu.VMEM((depth, lanes), BF16),
        ]

    def working(lanes):
        block = (Z_DEV, Y_DEV, depth, lanes)
        return [pltpu.VMEM(block, BF16)] + [pltpu.VMEM((2,) + block, BF16)] * 2

    return pl.pallas_call(
        fused_backward,
        grid=(4 * groups,),
        in_specs=[
            ANY_WHOLE, ANY_WHOLE, ANY_WHOLE, VMEM_WHOLE,
            pl.BlockSpec((step, D), lambda t: (group_and_block(jnp.maximum(t, 8))[1], 0)),
            VMEM_WHOLE, ANY_WHOLE, ANY_WHOLE, ANY_WHOLE, ANY_WHOLE, p_spec,
            ANY_WHOLE, ANY_WHOLE, ANY_WHOLE, ANY_WHOLE, ANY_WHOLE, ANY_WHOLE, VMEM_WHOLE,
        ],
        out_specs=[ANY_WHOLE] * 2 + [VMEM_WHOLE] * 5,
        out_shape=[
            shaped(BF16, groups, n, D), shaped(BF16, groups, n, D),
            shaped(F32, depth, 3 * width),
            shaped(F32, depth, width), shaped(F32, depth, hidden),
            shaped(F32, depth, hidden), shaped(F32, 16, D),
        ],
        scratch_shapes=[
            pltpu.VMEM((2, D, 3 * width), BF16), pltpu.VMEM((2, D, width), BF16),
            pltpu.VMEM((2, n, width), BF16), pltpu.VMEM((2, n, width), BF16),
            pltpu.VMEM((2, width, n), BF16), pltpu.VMEM((2, 8, n), F32),
            pltpu.VMEM((2, n, width), BF16),
            pltpu.VMEM((D, n), BF16), pltpu.VMEM((D, n), BF16), pltpu.VMEM((n, D), BF16),
            pltpu.VMEM((2, Z_DEV, depth, hidden), BF16),
            pltpu.VMEM((2, Z_DEV, Y_DEV, depth, hidden), BF16),
            pltpu.VMEM((2, n, width), BF16),
            pltpu.VMEM((2, 8, n), F32), pltpu.VMEM((2, 2, n, width), F32),
            pltpu.VMEM((2, n, 3 * width), BF16), pltpu.VMEM((n, D), F32),
            pltpu.VMEM((n, D), BF16), pltpu.VMEM((n, D), BF16), pltpu.VMEM((n, D), BF16),
            pltpu.VMEM((groups, 8, width), F32),
        ]
        + landing(hidden)[:1] + landing(hidden) + landing(hidden)
        + working(width) + landing(width)
        + working(3 * width) + landing(3 * width)
        + [
            pltpu.VMEM((4, 16, D), F32), pltpu.VMEM((6, 16, D), F32),
            pltpu.SemaphoreType.DMA((copies,)), pltpu.SemaphoreType.DMA((copies,)),
            pltpu.SemaphoreType.DMA((6,)), pltpu.SemaphoreType.DMA((2, 2, 4)),
            pltpu.SemaphoreType.DMA((2, 7)),
        ],
        compiler_params=pltpu.CompilerParams(
            vmem_limit_bytes=VMEM_LIMIT, collective_id=2, has_side_effects=True
        ),
        name="fused_backward",
    )(tokens, gq, gw, rows, dh1, gb, gbt, q, v, kt, p, scale, o, a1t, layer, fold, work, early)


def place_gradients(
    tie_ref, sums_ref, part0_ref, partw_ref, part1_ref, part2_ref, near_out_ref,
    near_grad_ref, far_out_ref, far_grad_ref, gains_ref, bias_ref, in_ref, out_ref, expand_ref,
    project_ref,
):
    far_out_ref[...] = near_out_ref[...]
    far_grad_ref[...] = near_grad_ref[...]
    own = gains_ref.shape[-1]
    width = partw_ref.shape[-1]

    @pl.when(pl.program_id(0) == 0)
    def _():
        first = (lax.axis_index("dp") * 4 + lax.axis_index("tensor")) * own
        feature = lax.broadcasted_iota(jnp.int32, (D, 128), 0)
        lane = lax.broadcasted_iota(jnp.int32, (D, 128), 1)
        chosen = ((feature == first + lane) & (lane < own)).astype(F32)
        sums = lax.dot_general(
            sums_ref[...], chosen, (((1,), (0,)), ((), ())),
            precision=lax.Precision.HIGHEST, preferred_element_type=F32,
        )[:, :own]
        s0, s1, s2, s3 = tie_ref[0], tie_ref[1], tie_ref[2], tie_ref[3]
        w_out = partw_ref[...].T

        def at(source, wanted, value):
            return jnp.where(source == wanted, value, jnp.zeros_like(value))

        row = lax.broadcasted_iota(jnp.int32, (NSRC, own), 0)
        for i, wanted in enumerate([s0, s0, s0, s1, s2, s3, s2, s2, s2, s2]):
            bias_ref[i] = jnp.where(row == wanted, sums[2 + i : 3 + i], 0.0)
        for s in range(NSRC):
            gains_ref[s, 0:1] = at(s, s0, sums[0:1])
            gains_ref[s, 1:2] = at(s, s2, sums[1:2])
            for j in range(3):
                in_ref[s, j] = at(s, s0, part0_ref[:, j * width : (j + 1) * width])
            out_ref[s] = at(s, s1, w_out)
            expand_ref[s] = at(s, s2, part1_ref[...])
            project_ref[s] = at(s, s3, part2_ref[...])


def run_place_gradients(tie, sums, part0, partw, part1, part2, out, grad, like):
    slots, n, _ = grad.shape
    gains, biases, w_in, w_out, w_expand, w_project = [item.shape for item in like]
    shapes = [
        gains, (biases[1], biases[0], biases[2]), w_in, w_out, w_expand,
        (w_project[0], w_project[2], w_project[1]),
    ]
    out, grad, gains, biases, w_in, w_out, w_expand, w_project = pl.pallas_call(
        place_gradients,
        grid=(slots,),
        in_specs=[SMEM_WHOLE] + [VMEM_WHOLE] * 5
        + [group(n, D), group(n, D)],
        out_specs=[group(n, D), group(n, D)] + [VMEM_WHOLE] * 6,
        out_shape=[shaped(BF16, slots, n, D)] * 2 + [shaped(F32, *item) for item in shapes],
        compiler_params=pltpu.CompilerParams(vmem_limit_bytes=VMEM_LIMIT),
        name="place_gradients",
    )(tie, sums, part0, partw, part1, part2, out, grad)
    biases = biases.transpose(1, 0, 2)
    return out, grad, gains, biases, w_in, w_out, w_expand, w_project.transpose(0, 2, 1)


def plain_step(
    tokens, lengths, tie_map, norm_gains, bias_rows, attention_in, attention_out,
    expand_weight, project_weight, cotangent,
):
    slot_rows = tokens.shape[0] // lengths.shape[0]
    me = lax.axis_index("tensor")
    in_local = lax.dynamic_index_in_dim(attention_in, tie_map[0], 0, keepdims=False)
    out_local = lax.dynamic_index_in_dim(attention_out, tie_map[1], 0, keepdims=False)
    expand_local = lax.dynamic_index_in_dim(expand_weight, tie_map[2], 0, keepdims=False)
    project_local = lax.dynamic_index_in_dim(project_weight, tie_map[3], 0, keepdims=False)
    local0 = jnp.concatenate([in_local, out_local.T[None]], 0)
    row_kinds = jnp.array([0, 0, 0, 1, 2, 3] + [2] * (FF // D), dtype=jnp.int32)
    gain_kinds = jnp.array([0, 2], dtype=jnp.int32)
    gain_pick = norm_gains[tie_map[gain_kinds], jnp.arange(2)]
    bias_pick = bias_rows[tie_map[row_kinds], jnp.arange(row_kinds.shape[0])]
    vectors = jnp.concatenate([gain_pick, bias_pick], 0)
    x = lax.dynamic_slice_in_dim(tokens, me * slot_rows, slot_rows, 0)
    cot = lax.dynamic_slice_in_dim(cotangent, me * slot_rows, slot_rows, 0)
    length = lax.dynamic_slice_in_dim(lengths, me, 1, 0)
    rows = lax.all_gather(vectors, ("dp", "tensor"), axis=1, tiled=True).astype(F32)
    rows = jnp.concatenate([rows, jnp.zeros((4, D), F32)], 0)

    def gathered(piece, axis):
        piece = lax.all_gather(piece, "dp", axis=axis, tiled=True)
        return lax.all_gather(piece, "tensor", axis=0)

    g0 = gathered(local0, 1)
    g1 = gathered(expand_local, 0)
    g2 = gathered(project_local.T, 0)
    groups, width = g0.shape[0], g0.shape[-1]
    bqv = rows[3:5].reshape(2, groups, width).transpose(1, 0, 2)
    q, v, kt, p, o, a1t, h1, a2, a2t = run_attention_forward(length, x, g0, rows, bqv)
    out, d1, d2, dh1, gb, gbt, sums = run_feed_forward(length, cot, a2, a2t, h1, g1, g2, rows)
    d0, xg, sums_in, sums_qv = run_attention_backward(
        x, g0, rows, dh1, gb, gbt, q, v, kt, p, o, a1t
    )
    layer_out = lax.all_gather(out, "tensor", axis=0, tiled=True)
    tokens_grad = lax.all_gather(xg, "tensor", axis=0, tiled=True)

    def scattered(piece, axis):
        piece = lax.psum_scatter(piece, "tensor", scatter_dimension=0)
        return lax.psum_scatter(piece, "dp", scatter_dimension=axis, tiled=True).astype(F32)

    part0 = scattered(d0, 1)
    part1 = scattered(d1, 0)
    part2 = scattered(d2, 0)
    qv = sums_qv[:, :2].transpose(1, 0, 2).reshape(2, D)
    sums = jnp.concatenate(
        [sums_in[0:1], sums[1:2], sums_in[1:2], qv, sums[5:12]], 0
    )
    sums = lax.psum_scatter(sums, ("dp", "tensor"), scatter_dimension=1, tiled=True)
    return layer_out, tokens_grad, *placed(tie_map, sums, part0, part1, part2)


def fused_step(
    tokens, lengths, tie_map, norm_gains, bias_rows, attention_in, attention_out,
    expand_weight, project_weight, cotangent,
):
    slots = lengths.shape[0]
    tokens = tokens.reshape(slots, -1, D)
    cotangent = cotangent.reshape(slots, -1, D)
    gq, gw, g1, g2, rows, q, v, kt, p, scale, o, a1t, h1, a2, a2t = run_fused_forward(
        tie_map, lengths, tokens, norm_gains, bias_rows, attention_in, attention_out,
        expand_weight, project_weight,
    )
    layer, fold, work, dh1, gb, gbt, early = run_fused_feed_forward(
        lengths, cotangent, a2, a2t, h1, g1, g2, rows
    )
    grad, out, part0, partw, part1, part2, sums = run_fused_backward(
        tokens, gq, gw, rows, dh1, gb, gbt, q, v, kt, p, scale, o, a1t, layer, fold,
        work, early,
    )
    out, grad, *placed_grads = run_place_gradients(
        tie_map, sums, part0, partw, part1, part2, out, grad,
        (norm_gains, bias_rows, attention_in, attention_out, expand_weight, project_weight),
    )
    return out.reshape(-1, D), grad.reshape(-1, D), *placed_grads


def placed(tie_map, sums, part0, part1, part2):
    source = jnp.arange(NSRC, dtype=jnp.int32)

    def place(piece, which):
        pick = (source == tie_map[which]).reshape((NSRC,) + (1,) * piece.ndim)
        return jnp.where(pick, piece[None], 0.0)

    def place_rows(piece, kinds):
        pick = source[:, None] == tie_map[jnp.array(kinds, dtype=jnp.int32)][None, :]
        return jnp.where(pick[:, :, None], piece[None], 0.0)

    return (
        place_rows(sums[:2], [0, 2]),
        place_rows(sums[2:], [0, 0, 0, 1, 2, 3] + [2] * (FF // D)),
        place(part0[:3], 0),
        place(part0[3].T, 1),
        place(part1, 2),
        place(part2.T, 3),
    )


def solution(mesh):
    fused = mesh.shape["dp"] == Z_DEV * Y_DEV and mesh.shape["tensor"] == X_DEV * C_DEV
    return jax.shard_map(
        fused_step if fused else plain_step,
        mesh=mesh,
        in_specs=(
            P("dp", None),
            P("dp"),
            P(),
            P(None, None, ("dp", "tensor")),
            P(None, None, ("dp", "tensor")),
            P(None, None, "dp", "tensor"),
            P(None, "tensor", "dp"),
            P(None, "dp", "tensor"),
            P(None, "tensor", "dp"),
            P("dp", None),
        ),
        out_specs=(
            P("dp", None),
            P("dp", None),
            P(None, None, ("dp", "tensor")),
            P(None, None, ("dp", "tensor")),
            P(None, None, "dp", "tensor"),
            P(None, "tensor", "dp"),
            P(None, "dp", "tensor"),
            P(None, "tensor", "dp"),
        ),
        check_vma=False,
    )
```

profile of v0, /device:TPU:0, one launch (start us, length us, event | category | flops | bytes accessed | tf_op | source)
XLA Modules:
  0.0 236.2 jit_solution(5454620261089897918)
XLA Ops:
  0.6 76.0 %fused_forward.1 = (bf16[4,768,576]{2,1,0:T(8,128)(2,1)}, bf16[4,768,192]{2,1,0:T(8,128)(2,1)}, bf16[4,4,2,96,768]{4,3,2,1,0:T(8,128)(2,1)}, bf16[4,4,2,96,768]{...) custom-call(s32[4]{0:T(128)} %tie_ref.3, ...), custom_call_target="tpu_custom_call" | custom-call | tf_op jit(solution)/shard_map/fused_forward/pallas_call | solution.py:815
  76.6 48.7 %fused_feed_forward.1 = (bf16[1024,768]{1,0:T(8,128)(2,1)}, bf16[2,4,96,768]{3,2,1,0:T(8,128)(2,1)}, bf16[2,4,2,96,768]{4,3,2,1,0:T(8,128)(2,1)}, f32[1024,768]{...) custom-call(s32[4]{0:T(128)} %len_ref.3, bf16[4,1024,768]{2,1,0:T(8,128)(2,1)} %bitcast.10, ...), custom_call_target="tpu_custom_call" | custom-call | tf_op jit(solution)/shard_map/fused_feed_forward/pallas_call | solution.py:1125
  125.4 99.4 %fused_backward.1 = (bf16[4,1024,768]{2,1,0:T(8,128)(2,1)}, bf16[4,1024,768]{2,1,0:T(8,128)(2,1)}, f32[96,576]{1,0:T(8,128)}, f32[96,192]{1,0:T(8,128)}, f32[96,...) custom-call(bf16[4,1024,768]{2,1,0:T(8,128)(2,1)} %bitcast.9, bf16[4,768,576]{2,1,0:T(8,128)(2,1)} %get-tuple-element.45.gq_in, ...), custom_call_target="tpu_custom_call" | custom-call | tf_op jit(solution)/shard_map/fused_backward/pallas_call | solution.py:1548
  224.8 11.2 %place_gradients.1 = (bf16[4,1024,768]{2,1,0:T(8,128)(2,1)}, bf16[4,1024,768]{2,1,0:T(8,128)(2,1)}, f32[4,2,24]{2,1,0:T(2,128)}, f32[10,4,24]{2,1,0:T(4,128)}, f...) custom-call(s32[4]{0:T(128)} %tie_ref.3, ...), custom_call_target="tpu_custom_call" | custom-call | tf_op jit(solution)/shard_map/place_gradients/pallas_call | solution.py:1640
where the time goes:
time: 236 us
  Pallas kernels  235 us (100%)
    pallas_call x1, Pallas kernels, run_fused_backward(): pl.pallas_call(fused_backward, grid=(4 * groups,), in_specs=[ANY_WHOLE, A...  99.4 us
    pallas_call x1, Pallas kernels, run_fused_forward(): pl.pallas_call(fused_forward, grid=(groups,), in_specs=[SMEM_WHOLE, SMEM_...  76 us
    pallas_call x1, Pallas kernels, run_fused_feed_forward(): pl.pallas_call(fused_feed_forward, grid=(groups,), in_specs=[SMEM_WHOLE,...  48.7 us
    pallas_call x1, Pallas kernels, run_place_gradients(): pl.pallas_call(place_gradients, grid=(slots,), in_specs=[SMEM_WHOLE] + [V...  11.2 us

commit v1 on v0

--- a/solution.py
+++ b/solution.py
@@ -457,21 +457,42 @@
         pl.semaphore_wait(barrier, len(others))
 
 
+class Pieces:
+    def __init__(self, whole, pieces):
+        self.whole, self.pieces = whole, pieces
+
+    def start(self):
+        for piece in self.pieces:
+            piece.start()
+
+    def wait_recv(self):
+        self.whole.wait_recv()
+
+    def wait_send(self):
+        self.whole.wait_send()
+
+
 class Links:
     def __init__(self, send_sem, recv_sem):
         self.send_sem, self.recv_sem = send_sem, recv_sem
         self.copies = []
 
-    def add(self, device, src, dst):
+    def add(self, device, src, dst, parts=1, axis=0):
         number = len(self.copies)
-        copy = pltpu.make_async_remote_copy(
-            src_ref=src,
-            dst_ref=dst,
-            send_sem=self.send_sem.at[number],
-            recv_sem=self.recv_sem.at[number],
-            device_id=device,
-            device_id_type=pl.DeviceIdType.MESH,
-        )
+
+        def make(src, dst):
+            return pltpu.make_async_remote_copy(
+                src_ref=src,
+                dst_ref=dst,
+                send_sem=self.send_sem.at[number],
+                recv_sem=self.recv_sem.at[number],
+                device_id=device,
+                device_id_type=pl.DeviceIdType.MESH,
+            )
+
+        size = src.shape[axis] // parts
+        cuts = [(slice(None),) * axis + (pl.ds(i * size, size),) for i in range(parts)]
+        copy = Pieces(make(src, dst), [make(src.at[cut], dst.at[cut]) for cut in cuts])
         self.copies.append(copy)
         return copy
 
@@ -505,33 +526,33 @@
         y, other = place.y, place.other_y
 
         def same(device, k, yy, to):
-            return links.add(device, full(k, every, yy), full(to, every, yy))
+            return links.add(device, full(k, every, yy), full(to, every, yy), Z_DEV)
 
         def along_z(k, yy, block):
             here, passed = full(k, place.z, yy), full(k, place.zs[2], yy)
             return [
-                links.add(place.to_z[1], block, here),
-                links.add(place.to_z[2], block, here),
-                links.add(place.to_z[1], passed, passed),
+                links.add(place.to_z[1], block, here, 2),
+                links.add(place.to_z[2], block, here, 2),
+                links.add(place.to_z[1], passed, passed, 2),
             ]
 
         self.z = along_z(0, y, own)
         if order == X_Z_Y:
-            self.first = [links.add(place.to_x, own, full(2, place.z, y))]
+            self.first = [links.add(place.to_x, own, full(2, place.z, y), 2)]
             self.far = along_z(2, y, full(2, place.z, y))
             blocks = [(0, y), (2, y), (0, other), (2, other)]
         else:
             blocks = [(0, y), (0, other), (2, y), (2, other)]
         if order == Y_Z_X:
-            self.first = [links.add(place.to_y, own, full(0, place.z, y))]
+            self.first = [links.add(place.to_y, own, full(0, place.z, y), 2)]
             self.far = along_z(0, other, full(0, place.z, other))
         if order == Z_Y_X and single:
             self.first = [same(place.to_y, 0, y, 0)]
         if order == Z_Y_X and not single:
-            self.first = [links.add(place.to_y, own, full(0, place.z, y))]
+            self.first = [links.add(place.to_y, own, full(0, place.z, y), 2)]
             for k in range(1, 4):
                 block = full(0, place.zs[k], y)
-                self.first.append(links.add(place.to_y, block, block))
+                self.first.append(links.add(place.to_y, block, block, 2))
         self.second = [
             same(place.to_y, k, yy, k) if order == X_Z_Y else same(place.to_x, k, yy, 2)
             for k, yy in blocks[: 2 if last else 1]
@@ -626,18 +647,17 @@
 
     plan = [
         (0, 0, lambda: (pass_own(segw), pass_first(seg1), relay_z(seg2.z), pass_first(seg2))),
-        (0, 3, lambda: (pass_first(segw), relay_z(seg1.z), pass_core(seg0, 0))),
+        (0, 2, lambda: (pass_first(segw), relay_z(seg1.z), pass_core(seg0, 0))),
         (1, 0, lambda: recv(seg0.core[:2])),
         (1, 1, lambda: relay_z(seg1.far)),
-        (1, 3, lambda: pass_core(seg0, 1)),
-        (1, 4, lambda: (recv(segw.core[:2]), pass_core(segw, 0), pass_own(seg2))),
+        (1, 2, lambda: (
+            pass_core(seg0, 1), recv(segw.core[:2]), pass_core(segw, 0), pass_own(seg2),
+        )),
         (2, 1, lambda: relay_z(seg2.far)),
-        (2, 2, lambda: pass_core(segw, 1)),
-        (2, 3, lambda: pass_own(seg1)),
+        (2, 2, lambda: (pass_core(segw, 1), pass_own(seg1))),
         (3, 0, lambda: (recv(seg0.core[2:]), pass_far(seg1), flush[0][0].start())),
-        (3, 2, lambda: (pass_second(seg2), flush[1][0].start())),
-        (3, 3, lambda: (pass_far(seg2), flush[1][2].start())),
-        (3, 4, lambda: recv(segw.core[2:])),
+        (3, 1, lambda: (pass_second(seg2), flush[1][0].start())),
+        (3, 2, lambda: (pass_far(seg2), flush[1][2].start(), recv(segw.core[2:]))),
     ]
 
     def serve(point):
@@ -751,11 +771,11 @@
             far = s[:first]
             top = jnp.maximum(top, jnp.max(far, 0, keepdims=True))
         e_near = jnp.exp((near - top).astype(BF16))
-        p_ref[0, h, first:last, first:last] = e_near
+        p_ref[0, h, b, first:last, :] = e_near
         o = dot_nn(vt_ref[h, :, first:last], e_near)
         if b:
             e_far = jnp.exp((far - top).astype(BF16))
-            p_ref[0, h, :first, first:last] = e_far
+            p_ref[0, h, b, :first, :] = e_far
             o += dot_nn(vt_ref[h, :, :first], e_far)
         scale = 1.0 / o[HEAD_DIM : HEAD_DIM + 1]
         scale_ref[0, h : h + 1, first:last] = scale
@@ -764,13 +784,13 @@
         ).astype(BF16)
 
     scale_ref[0, heads:, :] = jnp.zeros((scale_ref.shape[1] - heads, n), F32)
-    for h in range(heads):
-        s = scores(h, 0)
-        for b in range(n // step):
-            ahead = scores(h, b + 1) if b + 1 < n // step else None
-            attend(h, b, s)
-            s = ahead
-        serve(2 + h)
+    ready = [scores(h, 0) for h in range(heads)]
+    for b in range(n // step):
+        ahead = [scores(h, b + 1) for h in range(heads)] if b + 1 < n // step else None
+        for h in range(heads):
+            attend(h, b, ready[h])
+        ready = ahead
+    serve(2)
 
     gw_ref[0] = allw_ref[t].reshape(gw_ref.shape[1:])
     o = ot_ref[...].T
@@ -818,7 +838,7 @@
         in_specs=[SMEM_WHOLE, SMEM_WHOLE, ANY_WHOLE] + [VMEM_WHOLE] * 6,
         out_specs=[
             group(D, 3 * width), group(D, width), ANY_WHOLE, ANY_WHOLE, VMEM_WHOLE,
-            group(n, width), group(n, width), group(width, n), group(heads, n, n),
+            group(n, width), group(n, width), group(width, n), group(heads, n // 256, n, 256),
             group(8, n), group(n, width), ANY_WHOLE, ANY_WHOLE, ANY_WHOLE, ANY_WHOLE,
         ],
         out_shape=[
@@ -827,7 +847,7 @@
             shaped(BF16, groups, Z_DEV, Y_DEV, depth, hidden),
             shaped(F32, 16, D),
             shaped(BF16, groups, n, width), shaped(BF16, groups, n, width),
-            shaped(BF16, groups, width, n), shaped(BF16, groups, heads, n, n),
+            shaped(BF16, groups, width, n), shaped(BF16, groups, heads, n // 256, n, 256),
             shaped(F32, groups, 8, n), shaped(BF16, groups, n, width), shaped(BF16, D, n), shaped(F32, n, D),
             shaped(BF16, n, D), shaped(BF16, D, n),
         ],
@@ -858,16 +878,15 @@
 
 
 class Result:
-    def __init__(self, links, place, own_ref, passing_ref, out_ref, step, sem):
-        count = own_ref.shape[0] // step
+    def __init__(self, links, place, own_ref, passing_ref, out_ref, step, sem, count):
         self.x, self.core, self.far, self.keep, self.keep_far = [], [], [], [], []
         for i in range(count):
             rows = pl.ds(i * step, step)
             mine, theirs = out_ref.at[place.t, rows], out_ref.at[place.ts[2], rows]
             own, passing = own_ref.at[rows], passing_ref.at[rows]
-            self.x.append(links.add(place.to_x, own, passing))
-            self.core.append(links.add(place.to_core, own, mine))
-            self.far.append(links.add(place.to_core, passing, theirs))
+            self.x.append(links.add(place.to_x, own, passing, 4))
+            self.core.append(links.add(place.to_core, own, mine, 4))
+            self.far.append(links.add(place.to_core, passing, theirs, 4))
             self.keep.append(pltpu.make_async_copy(own, mine, sem.at[0, i]))
             self.keep_far.append(pltpu.make_async_copy(passing, theirs, sem.at[1, i]))
 
@@ -908,22 +927,26 @@
     links = Links(send_sem, recv_sem)
     y, other = place.y, place.other_y
     last = [
-        links.add(place.to_x, far1_ref.at[0, :, other], missing_ref.at[0, 0]),
-        links.add(place.to_y, far2_ref.at[2, :, y], missing_ref.at[1, 0]),
+        links.add(place.to_x, far1_ref.at[0, :, other], missing_ref.at[0, 0], Z_DEV),
+        links.add(place.to_y, far2_ref.at[2, :, y], missing_ref.at[1, 0], Z_DEV),
     ]
     last_core = [
-        links.add(place.to_core, missing_ref.at[i, 0], missing_ref.at[i, 1]) for i in range(2)
+        links.add(place.to_core, missing_ref.at[i, 0], missing_ref.at[i, 1], Z_DEV)
+        for i in range(2)
     ]
     third = [
-        links.add(place.to_core, far_ref.at[2, :, y], third_ref.at[i])
+        links.add(place.to_core, far_ref.at[2, :, y], third_ref.at[i], Z_DEV)
         for i, far_ref in enumerate([far1_ref, far2_ref])
     ]
     core = [
-        [links.add(place.to_core, stage_ref.at[i], land_ref.at[s, i]) for i in range(2)]
+        [
+            links.add(place.to_core, stage_ref.at[i], land_ref.at[s, i], Z_DEV) for i in range(2)
+        ]
         for s in range(2)
     ]
     cross = [
-        links.add(place.to_y, near_ref.at[i, :, other], cross_ref.at[i]) for i in range(2)
+        links.add(place.to_y, near_ref.at[i, :, other], cross_ref.at[i], Z_DEV)
+        for i in range(2)
     ]
     fetch = pltpu.make_async_copy(cot_ref.at[place.t], gf_ref, local_sem.at[0])
     gb_ref, gbt_ref, dh1_ref = gf_ref, gft_ref, da2_ref
@@ -1159,20 +1182,22 @@
         zs = place.zs
         self.y = {
             s: [
-                links.add(place.to_y, work(s, zs[j], place.other_y), cross_ref.at[s, zs[j]])
+                links.add(
+                    place.to_y, work(s, zs[j], place.other_y), cross_ref.at[s, zs[j]], 2
+                )
                 for j in (1, 3, 2, 0)
             ]
             for s in slots
         }
         self.z = [
             [
-                links.add(place.to_z[1], acc(s, zs[1]), far_ref.at[s, 0]),
-                links.add(place.to_z[1], acc(s, zs[3]), far_ref.at[s, 1]),
-                links.add(place.to_z[2], mid_ref.at[s, 1], far_ref.at[s, 2]),
+                links.add(place.to_z[1], acc(s, zs[1]), far_ref.at[s, 0], 2),
+                links.add(place.to_z[1], acc(s, zs[3]), far_ref.at[s, 1], 2),
+                links.add(place.to_z[2], mid_ref.at[s, 1], far_ref.at[s, 2], 2),
             ]
             for s in range(2)
         ]
-        self.x = links.add(place.to_x, last_ref, side_ref)
+        self.x = links.add(place.to_x, last_ref, side_ref, 2)
 
     def fold_y(self, s, half):
         for i, j in [(0, 1), (1, 3), (2, 2), (3, 0)][2 * half : 2 * half + 2]:
@@ -1230,8 +1255,8 @@
     k, i = group_and_block(t)
     mine = place.group(k)
     now = k % 2
-    out = Result(links, place, own_ref, passing_ref, out_ref, step, result_sem.at[0])
-    layer = Result(links, place, layer_ref, passlayer_ref, layerout_ref, step, result_sem.at[1])
+    out = Result(links, place, own_ref, passing_ref, out_ref, step, result_sem.at[0], 4)
+    layer = Result(links, place, layer_ref, passlayer_ref, layerout_ref, step, result_sem.at[1], 4)
     fetch = pltpu.make_async_copy(tokens_ref.at[place.t], own_ref, local_sem.at[0])
     fetch_layer, fetch_work, fetch_fold, fetch_gbt, fetch_a1t = [
         pltpu.make_async_copy(there, here, local_sem.at[1 + j])
@@ -1251,8 +1276,8 @@
             for j, (there, here) in enumerate(pairs)
         ]
 
-    corew = [links.add(place.to_core, stagew_ref, landw_ref.at[i]) for i in range(2)]
-    core0 = [links.add(place.to_core, stage0_ref, land0_ref.at[i]) for i in range(2)]
+    corew = [links.add(place.to_core, stagew_ref, landw_ref.at[i], Z_DEV) for i in range(2)]
+    core0 = [links.add(place.to_core, stage0_ref, land0_ref.at[i], Z_DEV) for i in range(2)]
     def half_done(i, *landing):
         return Reduce(
             links, place, lambda s, z, y: work_ref.at[i, z, y],
@@ -1296,7 +1321,6 @@
         start(seg1.z[0][:2], seg2.z[0][:2])
         bqv_ref[...] = jnp.zeros_like(bqv_ref)
         sums_ref[0] = early_ref[...]
-        da1_ref[...] = jnp.zeros_like(da1_ref)
         fetch_gbt.wait()
 
     def add_core():
@@ -1409,7 +1433,7 @@
             for h in range(heads):
                 low, high = h * HEAD_DIM, (h + 1) * HEAD_DIM
                 here = (lane >= low) & (lane < high)
-                p = p_ref[0, h, :last, :]
+                p = p_ref[0, h, 0, :last, :]
                 dp = dot_nt(v, jnp.where(here, do, jnp.zeros((), BF16)))
                 ds = p * (dp - delta_ref[now, h : h + 1, first:last]).astype(BF16)
                 part = dot_nn(p, do)
@@ -1431,7 +1455,10 @@
             dqkv_ref[now, first:last, 2 * width :] = dv
             bqv_ref[mine, 0:1, :] += jnp.sum(dq.astype(F32), 0, keepdims=True)
             bqv_ref[mine, 1:2, :] += jnp.sum(dv.astype(F32), 0, keepdims=True)
-            da1_ref[first:last, :] += dot_nt(dqkv_ref[now, first:last, :], gq_ref[now])
+
+            @pl.when(t >= 8)
+            def _():
+                da1_ref[first:last, :] += dot_nt(dqkv_ref[now, first:last, :], gq_ref[now])
 
     serve(1)
 
@@ -1460,6 +1487,14 @@
         def _():
             fetch.wait()
             fetch_a1t.wait()
+
+        @when(3)
+        def _():
+            da1_ref[...] = dot_nt(dqkv_ref[now], gq_ref[now])
+
+        @when(7)
+        def _():
+            da1_ref[...] += dot_nt(dqkv_ref[now], gq_ref[now])
 
         value = dot_nn(a1t_ref[...], dqkv_ref[now]).reshape(Z_DEV, Y_DEV, depth, 3 * width)
         for s in range(2):
@@ -1528,8 +1563,8 @@
     step = n // 4
 
     p_spec = pl.BlockSpec(
-        (1, heads, n, step),
-        lambda t: (group_and_block(t)[0], 0, 0, group_and_block(t)[1]),
+        (1, heads, 1, n, step),
+        lambda t: (group_and_block(t)[0], 0, group_and_block(t)[1], 0, 0),
     )
 
     copies = 2 * 12 + 4 + 2 * 15 + 2 * 11 + 6

time: 236 us -> 238 us (level)
  no operation moved by 1% of the time
where the time goes in v1:
time: 238 us
  Pallas kernels  237 us (100%)
    pallas_call x1, Pallas kernels, run_fused_backward(): pl.pallas_call(fused_backward, grid=(4 * groups,), in_specs=[ANY_WHOLE, A...  101 us
    pallas_call x1, Pallas kernels, run_fused_forward(): pl.pallas_call(fused_forward, grid=(groups,), in_specs=[SMEM_WHOLE, SMEM_...  75.7 us
    pallas_call x1, Pallas kernels, run_fused_feed_forward(): pl.pallas_call(fused_feed_forward, grid=(groups,), in_specs=[SMEM_WHOLE,...  49 us
    pallas_call x1, Pallas kernels, run_place_gradients(): pl.pallas_call(place_gradients, grid=(slots,), in_specs=[SMEM_WHOLE] + [V...  11.2 us

profile of v1, /device:TPU:0, one launch (start us, length us, event | category | flops | bytes accessed | tf_op | source)
XLA Modules:
  0.0 237.6 jit_solution(11290318160402996693)
XLA Ops:
  0.6 75.7 %fused_forward.1 = (bf16[4,768,576]{2,1,0:T(8,128)(2,1)}, bf16[4,768,192]{2,1,0:T(8,128)(2,1)}, bf16[4,4,2,96,768]{4,3,2,1,0:T(8,128)(2,1)}, bf16[4,4,2,96,768]{...) custom-call(s32[4]{0:T(128)} %tie_ref.3, ...), custom_call_target="tpu_custom_call" | custom-call | tf_op jit(solution)/shard_map/fused_forward/pallas_call | solution.py:835
  76.4 49.0 %fused_feed_forward.1 = (bf16[1024,768]{1,0:T(8,128)(2,1)}, bf16[2,4,96,768]{3,2,1,0:T(8,128)(2,1)}, bf16[2,4,2,96,768]{4,3,2,1,0:T(8,128)(2,1)}, f32[1024,768]{...) custom-call(s32[4]{0:T(128)} %len_ref.3, bf16[4,1024,768]{2,1,0:T(8,128)(2,1)} %bitcast.10, ...), custom_call_target="tpu_custom_call" | custom-call | tf_op jit(solution)/shard_map/fused_feed_forward/pallas_call | solution.py:1148
  125.3 100.9 %fused_backward.1 = (bf16[4,1024,768]{2,1,0:T(8,128)(2,1)}, bf16[4,1024,768]{2,1,0:T(8,128)(2,1)}, f32[96,576]{1,0:T(8,128)}, f32[96,192]{1,0:T(8,128)}, f32[96,...) custom-call(bf16[4,1024,768]{2,1,0:T(8,128)(2,1)} %bitcast.9, bf16[4,768,576]{2,1,0:T(8,128)(2,1)} %get-tuple-element.45.gq_in, ...), custom_call_target="tpu_custom_call" | custom-call | tf_op jit(solution)/shard_map/fused_backward/pallas_call | solution.py:1583
  226.2 11.2 %place_gradients.1 = (bf16[4,1024,768]{2,1,0:T(8,128)(2,1)}, bf16[4,1024,768]{2,1,0:T(8,128)(2,1)}, f32[4,2,24]{2,1,0:T(2,128)}, f32[10,4,24]{2,1,0:T(4,128)}, f...) custom-call(s32[4]{0:T(128)} %tie_ref.3, ...), custom_call_target="tpu_custom_call" | custom-call | tf_op jit(solution)/shard_map/place_gradients/pallas_call | solution.py:1675

commit v2 on v1

--- a/solution.py
+++ b/solution.py
@@ -531,12 +531,13 @@
         def along_z(k, yy, block):
             here, passed = full(k, place.z, yy), full(k, place.zs[2], yy)
             return [
-                links.add(place.to_z[1], block, here, 2),
-                links.add(place.to_z[2], block, here, 2),
-                links.add(place.to_z[1], passed, passed, 2),
+                links.add(place.to_z[1], block, here),
+                links.add(place.to_z[2], block, here),
+                links.add(place.to_z[1], passed, passed),
             ]
 
-        self.z = along_z(0, y, own)
+        if order != WHOLE:
+            self.z = along_z(0, y, own)
         if order == X_Z_Y:
             self.first = [links.add(place.to_x, own, full(2, place.z, y), 2)]
             self.far = along_z(2, y, full(2, place.z, y))
@@ -549,10 +550,11 @@
         if order == Z_Y_X and single:
             self.first = [same(place.to_y, 0, y, 0)]
         if order == Z_Y_X and not single:
-            self.first = [links.add(place.to_y, own, full(0, place.z, y), 2)]
+            self.first = [links.add(place.to_y, own, full(0, place.z, y))]
             for k in range(1, 4):
                 block = full(0, place.zs[k], y)
-                self.first.append(links.add(place.to_y, block, block, 2))
+                self.first.append(links.add(place.to_y, block, block))
+            return
         self.second = [
             same(place.to_y, k, yy, k) if order == X_Z_Y else same(place.to_x, k, yy, 2)
             for k, yy in blocks[: 2 if last else 1]
@@ -562,7 +564,7 @@
         self.core = [same(place.to_core, k, yy, k + 1) for k, yy in blocks]
 
 
-Z_Y_X, Y_Z_X, X_Z_Y = range(3)
+Z_Y_X, Y_Z_X, X_Z_Y, WHOLE = range(4)
 
 
 def fused_forward(
@@ -574,7 +576,7 @@
     all0_ref, allw_ref, w1_ref, w2_ref, vecs_ref, bqv_ref, x_ref, a1_ref, k_ref, qa_ref, vt_ref, ot_ref, a1t_ref, h1_ref, a2_ref, a2t_ref,
     send_sem, recv_sem, local_sem, flush_sem, row_sem,
 ):
-    t = pl.program_id(0)
+    t, h = pl.program_id(0), pl.program_id(1)
     n, _ = x_ref.shape
     width = allw_ref.shape[-1]
     heads = width // HEAD_DIM
@@ -587,9 +589,15 @@
     column = vecs_ref.at[:, :, x, c]
     vec_one = [links.add(device, vec_ref, mine_there) for device in place.same_t]
     vec_two = [links.add(device, column, column) for device in place.same_dp]
-    seg0 = Gather(
-        links, place, own0_ref, lambda k, z, y: all0_ref.at[k, z, y], Z_Y_X, single=False
-    )
+    half = own0_ref.shape[0] // 2
+    halves = []
+    for i in range(2):
+        rows = pl.ds(i * half, half)
+        halves.append(Gather(
+            links, place, own0_ref.at[rows],
+            lambda k, z, y, rows=rows: all0_ref.at[k, z, y, rows], Z_Y_X, single=False,
+        ))
+    seg0 = Gather(links, place, own0_ref, lambda k, z, y: all0_ref.at[k, z, y], WHOLE)
     segw = Gather(links, place, ownw_ref, lambda k, z, y: allw_ref.at[k, z, y], Z_Y_X)
     seg1 = Gather(
         links, place, own1_ref, lambda k, z, y: w1_ref.at[k, z, y], Y_Z_X, last=False
@@ -647,25 +655,27 @@
 
     plan = [
         (0, 0, lambda: (pass_own(segw), pass_first(seg1), relay_z(seg2.z), pass_first(seg2))),
-        (0, 2, lambda: (pass_first(segw), relay_z(seg1.z), pass_core(seg0, 0))),
+        (0, 3, lambda: (pass_first(segw), relay_z(seg1.z), pass_core(seg0, 0))),
         (1, 0, lambda: recv(seg0.core[:2])),
         (1, 1, lambda: relay_z(seg1.far)),
-        (1, 2, lambda: (
-            pass_core(seg0, 1), recv(segw.core[:2]), pass_core(segw, 0), pass_own(seg2),
-        )),
+        (1, 3, lambda: pass_core(seg0, 1)),
+        (1, 4, lambda: (recv(segw.core[:2]), pass_core(segw, 0), pass_own(seg2))),
         (2, 1, lambda: relay_z(seg2.far)),
-        (2, 2, lambda: (pass_core(segw, 1), pass_own(seg1))),
+        (2, 2, lambda: pass_core(segw, 1)),
+        (2, 3, lambda: pass_own(seg1)),
         (3, 0, lambda: (recv(seg0.core[2:]), pass_far(seg1), flush[0][0].start())),
-        (3, 1, lambda: (pass_second(seg2), flush[1][0].start())),
-        (3, 2, lambda: (pass_far(seg2), flush[1][2].start(), recv(segw.core[2:]))),
+        (3, 2, lambda: (pass_second(seg2), flush[1][0].start())),
+        (3, 3, lambda: (pass_far(seg2), flush[1][2].start())),
+        (3, 4, lambda: recv(segw.core[2:])),
     ]
 
-    def serve(point):
+    def serve(points):
         for step, where, act in plan:
-            if where == point:
-                pl.when(t == step)(lambda act=act: (act(), None)[1])
-
-    @pl.when(t == 0)
+            if where in points:
+                now = (t == step) & (h == max(where - 2, 0))
+                pl.when(now)(lambda act=act: (act(), None)[1])
+
+    @pl.when((t == 0) & (h == 0))
     def _():
         s0, s1, s2, s3 = tie_ref[0], tie_ref[1], tie_ref[2], tie_ref[3]
         fetch.start()
@@ -684,7 +694,9 @@
         for j in range(3):
             own0_ref[:, j * width : (j + 1) * width] = in_ref[s0, j]
         place.greet(place.same_t + place.same_dp)
-        start(vec_one, seg0.z[1], seg0.z[0], seg0.first[0])
+        start(vec_one)
+        for part in halves:
+            start(part.z[1], part.z[0], part.first[0])
         vecs_ref[z, y, x, c] = vec_ref[...]
         ones = lax.broadcasted_iota(jnp.int32, (vt_ref.shape[1] - HEAD_DIM, n), 0) == 0
         for h in range(heads):
@@ -698,16 +710,21 @@
         w2_ref[0, z, y] = own2_ref[...]
         recv(vec_one)
         start(vec_two)
-        relay_z(seg0.z)
-        start(seg0.first[2])
-        recv(seg0.z[0])
-        start(seg0.first[1], segw.z[1], segw.z[0], seg2.z[1])
+        for part in halves:
+            relay_z(part.z)
+            start(part.first[2])
+        for part in halves:
+            recv(part.z[0])
+            start(part.first[1])
+        start(segw.z[1], segw.z[0], seg2.z[1])
         recv(vec_two)
         start(seg2.first)
         vecs = vecs_ref[...].reshape(D, vecs_ref.shape[-1]).T[:16]
         rows_ref[...] = vecs
-        recv(seg0.z[2])
-        start(seg0.first[3], seg1.first, seg0.second[0], seg0.core[0])
+        for part in halves:
+            recv(part.z[2])
+            start(part.first[3])
+        start(seg1.first, seg0.second[0], seg0.core[0])
         for k in range(4):
             part = slice(k * width, (k + 1) * width)
             bqv_ref[k, 0:1, :width] = vecs[3:4, part]
@@ -728,76 +745,82 @@
         put_a1t.start()
         relay_z(segw.z)
         start(seg2.z[0], seg1.z[1], seg1.z[0])
-        recv(seg0.first)
+        recv(halves[0].first, halves[1].first)
         start(seg0.second[1], seg0.core[1])
 
-    serve(0)
-    gq = all0_ref[t].reshape(D, 3 * width)
-    gq_ref[0] = gq
-    mine = place.group(t)
-    qkv = dot_nn(a1_ref[...], gq) + bqv_ref[mine, 0:1, :]
-    q = qkv[:, :width].astype(BF16) * jnp.asarray(HEAD_DIM ** -0.5, BF16)
-    k = qkv[:, width : 2 * width].astype(BF16)
-    v = qkv[:, 2 * width :].astype(BF16)
-    q_ref[0] = q
-    kt_ref[0] = k.T
-    v_ref[0] = v
-    vt = v.T
-    for h in range(heads):
-        vt_ref[h, :HEAD_DIM, :] = vt[h * HEAD_DIM : (h + 1) * HEAD_DIM]
-    spare = k_ref.shape[1] - width
-    dead = lax.broadcasted_iota(jnp.int32, (n, spare), 0) >= length
-    first_column = lax.broadcasted_iota(jnp.int32, (n, spare), 1) == 0
-    k_ref[:, :width] = k
-    k_ref[:, width:] = jnp.where(first_column & dead, MASKED, 0.0).astype(BF16)
-    qa_ref[:, :width] = q
-    qa_ref[:, width:] = jnp.where(first_column, 1.0, 0.0).astype(BF16)
-
-    serve(1)
-    def scores(h, b):
+    serve([0])
+
+    @pl.when(h == 0)
+    def _():
+        gq = all0_ref[t].reshape(D, 3 * width)
+        gq_ref[0] = gq
+        mine = place.group(t)
+        qkv = dot_nn(a1_ref[...], gq) + bqv_ref[mine, 0:1, :]
+        q = qkv[:, :width].astype(BF16) * jnp.asarray(HEAD_DIM ** -0.5, BF16)
+        k = qkv[:, width : 2 * width].astype(BF16)
+        v = qkv[:, 2 * width :].astype(BF16)
+        q_ref[0] = q
+        kt_ref[0] = k.T
+        v_ref[0] = v
+        vt = v.T
+        for h in range(heads):
+            vt_ref[h, :HEAD_DIM, :] = vt[h * HEAD_DIM : (h + 1) * HEAD_DIM]
+        spare = k_ref.shape[1] - width
+        dead = lax.broadcasted_iota(jnp.int32, (n, spare), 0) >= length
+        first_column = lax.broadcasted_iota(jnp.int32, (n, spare), 1) == 0
+        k_ref[:, :width] = k
+        k_ref[:, width:] = jnp.where(first_column & dead, MASKED, 0.0).astype(BF16)
+        qa_ref[:, :width] = q
+        qa_ref[:, width:] = jnp.where(first_column, 1.0, 0.0).astype(BF16)
+        scale_ref[0, heads:, :] = jnp.zeros((scale_ref.shape[1] - heads, n), F32)
+
+    serve([1])
+
+    lane = lax.broadcasted_iota(jnp.int32, (1, qa_ref.shape[1]), 1)
+    keep = ((lane >= h * HEAD_DIM) & (lane < (h + 1) * HEAD_DIM)) | (lane >= width)
+    key = lax.broadcasted_iota(jnp.int32, (step, step), 0)
+    query = lax.broadcasted_iota(jnp.int32, (step, step), 1)
+    head = pl.ds(pl.multiple_of(h * HEAD_DIM, HEAD_DIM), HEAD_DIM)
+
+    def scores(b):
         first, last = b * step, (b + 1) * step
-        q = qa_ref[first:last, :]
-        lane = lax.broadcasted_iota(jnp.int32, (1, q.shape[1]), 1)
-        keep = head_mask((1, q.shape[1]), h) | (lane >= width)
-        return dot_nt(k_ref[:last, :], jnp.where(keep, q, jnp.zeros((), BF16)))
-
-    def attend(h, b, s):
+        q = jnp.where(keep, qa_ref[first:last, :], jnp.zeros((), BF16))
+        return dot_nt(k_ref[:last, :], q)
+
+    def attend(b, s):
         first, last = b * step, (b + 1) * step
-        key = lax.broadcasted_iota(jnp.int32, (step, step), 0)
-        query = lax.broadcasted_iota(jnp.int32, (step, step), 1)
         near = jnp.where(key <= query, s[first:], MASKED)
         top = jnp.max(near, 0, keepdims=True)
         if b:
             far = s[:first]
             top = jnp.maximum(top, jnp.max(far, 0, keepdims=True))
         e_near = jnp.exp((near - top).astype(BF16))
-        p_ref[0, h, b, first:last, :] = e_near
+        p_ref[0, 0, b, first:last, :] = e_near
         o = dot_nn(vt_ref[h, :, first:last], e_near)
         if b:
             e_far = jnp.exp((far - top).astype(BF16))
-            p_ref[0, h, b, :first, :] = e_far
+            p_ref[0, 0, b, :first, :] = e_far
             o += dot_nn(vt_ref[h, :, :first], e_far)
         scale = 1.0 / o[HEAD_DIM : HEAD_DIM + 1]
-        scale_ref[0, h : h + 1, first:last] = scale
-        ot_ref[h * HEAD_DIM : (h + 1) * HEAD_DIM, first:last] = (
-            o[:HEAD_DIM] * scale
-        ).astype(BF16)
-
-    scale_ref[0, heads:, :] = jnp.zeros((scale_ref.shape[1] - heads, n), F32)
-    ready = [scores(h, 0) for h in range(heads)]
+        scale_ref[0, pl.ds(h, 1), first:last] = scale
+        ot_ref[head, first:last] = (o[:HEAD_DIM] * scale).astype(BF16)
+
+    s = scores(0)
     for b in range(n // step):
-        ahead = [scores(h, b + 1) for h in range(heads)] if b + 1 < n // step else None
-        for h in range(heads):
-            attend(h, b, ready[h])
-        ready = ahead
-    serve(2)
-
-    gw_ref[0] = allw_ref[t].reshape(gw_ref.shape[1:])
-    o = ot_ref[...].T
-    o_ref[0] = o
-    h1_ref[...] += dot_nt(o, gw_ref[0])
-
-    @pl.when(t == 3)
+        ahead = scores(b + 1) if b + 1 < n // step else None
+        attend(b, s)
+        s = ahead
+
+    serve([2, 3, 4])
+
+    @pl.when(h == heads - 1)
+    def _():
+        gw_ref[0] = allw_ref[t].reshape(gw_ref.shape[1:])
+        o = ot_ref[...].T
+        o_ref[0] = o
+        h1_ref[...] += dot_nt(o, gw_ref[0])
+
+    @pl.when((t == 3) & (h == heads - 1))
     def _():
         for i, rows in enumerate(blocks(n, step)):
             xhat, _ = norm_parts(h1_ref[rows, :])
@@ -819,7 +842,7 @@
                 copy.wait()
 
 
-N_GATHER = 10 + 13 + 10 + 10 + 10
+N_GATHER = 10 + 14 + 6 + 10 + 10 + 10
 VMEM_WHOLE = pl.BlockSpec(memory_space=pltpu.VMEM)
 ANY_WHOLE = pl.BlockSpec(memory_space=pl.ANY)
 
@@ -832,13 +855,18 @@
     w_project = w_project.transpose(0, 2, 1)
     biases = biases.transpose(1, 0, 2)
     own = gains.shape[-1]
+
+    def group(*shape):
+        return pl.BlockSpec((1,) + shape, lambda t, h: (t,) + (0,) * len(shape))
+
+    per_head = pl.BlockSpec((1, 1, n // 256, n, 256), lambda t, h: (t, h, 0, 0, 0))
     return pl.pallas_call(
         fused_forward,
-        grid=(groups,),
+        grid=(groups, heads),
         in_specs=[SMEM_WHOLE, SMEM_WHOLE, ANY_WHOLE] + [VMEM_WHOLE] * 6,
         out_specs=[
             group(D, 3 * width), group(D, width), ANY_WHOLE, ANY_WHOLE, VMEM_WHOLE,
-            group(n, width), group(n, width), group(width, n), group(heads, n // 256, n, 256),
+            group(n, width), group(n, width), group(width, n), per_head,
             group(8, n), group(n, width), ANY_WHOLE, ANY_WHOLE, ANY_WHOLE, ANY_WHOLE,
         ],
         out_shape=[
@@ -884,9 +912,9 @@
             rows = pl.ds(i * step, step)
             mine, theirs = out_ref.at[place.t, rows], out_ref.at[place.ts[2], rows]
             own, passing = own_ref.at[rows], passing_ref.at[rows]
-            self.x.append(links.add(place.to_x, own, passing, 4))
-            self.core.append(links.add(place.to_core, own, mine, 4))
-            self.far.append(links.add(place.to_core, passing, theirs, 4))
+            self.x.append(links.add(place.to_x, own, passing))
+            self.core.append(links.add(place.to_core, own, mine))
+            self.far.append(links.add(place.to_core, passing, theirs))
             self.keep.append(pltpu.make_async_copy(own, mine, sem.at[0, i]))
             self.keep_far.append(pltpu.make_async_copy(passing, theirs, sem.at[1, i]))
 
@@ -927,26 +955,22 @@
     links = Links(send_sem, recv_sem)
     y, other = place.y, place.other_y
     last = [
-        links.add(place.to_x, far1_ref.at[0, :, other], missing_ref.at[0, 0], Z_DEV),
-        links.add(place.to_y, far2_ref.at[2, :, y], missing_ref.at[1, 0], Z_DEV),
+        links.add(place.to_x, far1_ref.at[0, :, other], missing_ref.at[0, 0]),
+        links.add(place.to_y, far2_ref.at[2, :, y], missing_ref.at[1, 0]),
     ]
     last_core = [
-        links.add(place.to_core, missing_ref.at[i, 0], missing_ref.at[i, 1], Z_DEV)
-        for i in range(2)
+        links.add(place.to_core, missing_ref.at[i, 0], missing_ref.at[i, 1]) for i in range(2)
     ]
     third = [
-        links.add(place.to_core, far_ref.at[2, :, y], third_ref.at[i], Z_DEV)
+        links.add(place.to_core, far_ref.at[2, :, y], third_ref.at[i])
         for i, far_ref in enumerate([far1_ref, far2_ref])
     ]
     core = [
-        [
-            links.add(place.to_core, stage_ref.at[i], land_ref.at[s, i], Z_DEV) for i in range(2)
-        ]
+        [links.add(place.to_core, stage_ref.at[i], land_ref.at[s, i]) for i in range(2)]
         for s in range(2)
     ]
     cross = [
-        links.add(place.to_y, near_ref.at[i, :, other], cross_ref.at[i], Z_DEV)
-        for i in range(2)
+        links.add(place.to_y, near_ref.at[i, :, other], cross_ref.at[i]) for i in range(2)
     ]
     fetch = pltpu.make_async_copy(cot_ref.at[place.t], gf_ref, local_sem.at[0])
     gb_ref, gbt_ref, dh1_ref = gf_ref, gft_ref, da2_ref
@@ -1183,7 +1207,7 @@
         self.y = {
             s: [
                 links.add(
-                    place.to_y, work(s, zs[j], place.other_y), cross_ref.at[s, zs[j]], 2
+                    place.to_y, work(s, zs[j], place.other_y), cross_ref.at[s, zs[j]]
                 )
                 for j in (1, 3, 2, 0)
             ]
@@ -1191,13 +1215,13 @@
         }
         self.z = [
             [
-                links.add(place.to_z[1], acc(s, zs[1]), far_ref.at[s, 0], 2),
-                links.add(place.to_z[1], acc(s, zs[3]), far_ref.at[s, 1], 2),
-                links.add(place.to_z[2], mid_ref.at[s, 1], far_ref.at[s, 2], 2),
+                links.add(place.to_z[1], acc(s, zs[1]), far_ref.at[s, 0]),
+                links.add(place.to_z[1], acc(s, zs[3]), far_ref.at[s, 1]),
+                links.add(place.to_z[2], mid_ref.at[s, 1], far_ref.at[s, 2]),
             ]
             for s in range(2)
         ]
-        self.x = links.add(place.to_x, last_ref, side_ref, 2)
+        self.x = links.add(place.to_x, last_ref, side_ref)
 
     def fold_y(self, s, half):
         for i, j in [(0, 1), (1, 3), (2, 2), (3, 0)][2 * half : 2 * half + 2]:
@@ -1276,8 +1300,8 @@
             for j, (there, here) in enumerate(pairs)
         ]
 
-    corew = [links.add(place.to_core, stagew_ref, landw_ref.at[i], Z_DEV) for i in range(2)]
-    core0 = [links.add(place.to_core, stage0_ref, land0_ref.at[i], Z_DEV) for i in range(2)]
+    corew = [links.add(place.to_core, stagew_ref, landw_ref.at[i]) for i in range(2)]
+    core0 = [links.add(place.to_core, stage0_ref, land0_ref.at[i]) for i in range(2)]
     def half_done(i, *landing):
         return Reduce(
             links, place, lambda s, z, y: work_ref.at[i, z, y],
@@ -1462,6 +1486,36 @@
 
     serve(1)
 
+    @pl.when((t == 3) | (t == 7) | (t > 13))
+    def _():
+        @when(3)
+        def _():
+            fetch.wait()
+            fetch_a1t.wait()
+
+        @when(3)
+        def _():
+            da1_ref[...] = dot_nt(dqkv_ref[now], gq_ref[now])
+
+        @when(7)
+        def _():
+            da1_ref[...] += dot_nt(dqkv_ref[now], gq_ref[now])
+
+        value = dot_nn(a1t_ref[...], dqkv_ref[now]).reshape(Z_DEV, Y_DEV, depth, 3 * width)
+        for s in range(2):
+            @when(3 + 11 * s)
+            def _():
+                if s:
+                    core0[0].wait_send()
+                stage0_ref[...] = value.astype(BF16)
+                start(core0[s])
+
+            @when(7 + 8 * s)
+            def _():
+                recv(core0[s])
+                work0_ref[s] = (value + land0_ref[s].astype(F32)).astype(BF16)
+                start(seg0.y[s])
+
     @pl.when((t > 8) & (t % 2 == 1))
     def _():
         rows = pl.ds(pl.multiple_of(i * step, step), step)
@@ -1480,36 +1534,6 @@
             @pl.when(i == ii)
             def _():
                 out.send(ii)
-
-    @pl.when((t == 3) | (t == 7) | (t > 13))
-    def _():
-        @when(3)
-        def _():
-            fetch.wait()
-            fetch_a1t.wait()
-
-        @when(3)
-        def _():
-            da1_ref[...] = dot_nt(dqkv_ref[now], gq_ref[now])
-
-        @when(7)
-        def _():
-            da1_ref[...] += dot_nt(dqkv_ref[now], gq_ref[now])
-
-        value = dot_nn(a1t_ref[...], dqkv_ref[now]).reshape(Z_DEV, Y_DEV, depth, 3 * width)
-        for s in range(2):
-            @when(3 + 11 * s)
-            def _():
-                if s:
-                    core0[0].wait_send()
-                stage0_ref[...] = value.astype(BF16)
-                start(core0[s])
-
-            @when(7 + 8 * s)
-            def _():
-                recv(core0[s])
-                work0_ref[s] = (value + land0_ref[s].astype(F32)).astype(BF16)
-                start(seg0.y[s])
 
     @when(15)
     def _():
@@ -1629,40 +1653,42 @@
 def place_gradients(
     tie_ref, sums_ref, part0_ref, partw_ref, part1_ref, part2_ref, near_out_ref,
     near_grad_ref, far_out_ref, far_grad_ref, gains_ref, bias_ref, in_ref, out_ref, expand_ref,
-    project_ref,
+    project_ref, chosen_ref,
 ):
+    t = pl.program_id(0)
     far_out_ref[...] = near_out_ref[...]
     far_grad_ref[...] = near_grad_ref[...]
     own = gains_ref.shape[-1]
     width = partw_ref.shape[-1]
-
-    @pl.when(pl.program_id(0) == 0)
+    kinds = [tie_ref[0], tie_ref[1], tie_ref[2], tie_ref[3]]
+
+    @pl.when(t == 0)
     def _():
         first = (lax.axis_index("dp") * 4 + lax.axis_index("tensor")) * own
         feature = lax.broadcasted_iota(jnp.int32, (D, 128), 0)
         lane = lax.broadcasted_iota(jnp.int32, (D, 128), 1)
         chosen = ((feature == first + lane) & (lane < own)).astype(F32)
-        sums = lax.dot_general(
+        chosen_ref[...] = lax.dot_general(
             sums_ref[...], chosen, (((1,), (0,)), ((), ())),
             precision=lax.Precision.HIGHEST, preferred_element_type=F32,
-        )[:, :own]
-        s0, s1, s2, s3 = tie_ref[0], tie_ref[1], tie_ref[2], tie_ref[3]
-        w_out = partw_ref[...].T
-
-        def at(source, wanted, value):
-            return jnp.where(source == wanted, value, jnp.zeros_like(value))
-
+        )
         row = lax.broadcasted_iota(jnp.int32, (NSRC, own), 0)
-        for i, wanted in enumerate([s0, s0, s0, s1, s2, s3, s2, s2, s2, s2]):
-            bias_ref[i] = jnp.where(row == wanted, sums[2 + i : 3 + i], 0.0)
-        for s in range(NSRC):
-            gains_ref[s, 0:1] = at(s, s0, sums[0:1])
-            gains_ref[s, 1:2] = at(s, s2, sums[1:2])
-            for j in range(3):
-                in_ref[s, j] = at(s, s0, part0_ref[:, j * width : (j + 1) * width])
-            out_ref[s] = at(s, s1, w_out)
-            expand_ref[s] = at(s, s2, part1_ref[...])
-            project_ref[s] = at(s, s3, part2_ref[...])
+        for i, kind in enumerate([0, 0, 0, 1, 2, 3, 2, 2, 2, 2]):
+            value = chosen_ref[2 + i : 3 + i, :own]
+            bias_ref[i] = jnp.where(row == kinds[kind], value, 0.0)
+
+    @pl.when(t < NSRC)
+    def _():
+        def here(kind, value):
+            return jnp.where(kinds[kind] == t, value, jnp.zeros_like(value))
+
+        gains_ref[0, 0:1] = here(0, chosen_ref[0:1, :own])
+        gains_ref[0, 1:2] = here(2, chosen_ref[1:2, :own])
+        for j in range(3):
+            in_ref[0, j] = here(0, part0_ref[:, j * width : (j + 1) * width])
+        out_ref[0] = here(1, partw_ref[...].T)
+        expand_ref[0] = here(2, part1_ref[...])
+        project_ref[0] = here(3, part2_ref[...])
 
 
 def run_place_gradients(tie, sums, part0, partw, part1, part2, out, grad, like):
@@ -1672,13 +1698,20 @@
         gains, (biases[1], biases[0], biases[2]), w_in, w_out, w_expand,
         (w_project[0], w_project[2], w_project[1]),
     ]
+
+    def source(shape):
+        return pl.BlockSpec(
+            (1,) + shape[1:], lambda t: (jnp.minimum(t, NSRC - 1),) + (0,) * (len(shape) - 1)
+        )
+
     out, grad, gains, biases, w_in, w_out, w_expand, w_project = pl.pallas_call(
         place_gradients,
         grid=(slots,),
-        in_specs=[SMEM_WHOLE] + [VMEM_WHOLE] * 5
-        + [group(n, D), group(n, D)],
-        out_specs=[group(n, D), group(n, D)] + [VMEM_WHOLE] * 6,
+        in_specs=[SMEM_WHOLE] + [VMEM_WHOLE] * 5 + [group(n, D), group(n, D)],
+        out_specs=[group(n, D), group(n, D), source(shapes[0]), VMEM_WHOLE]
+        + [source(shape) for shape in shapes[2:]],
         out_shape=[shaped(BF16, slots, n, D)] * 2 + [shaped(F32, *item) for item in shapes],
+        scratch_shapes=[pltpu.VMEM((16, 128), F32)],
         compiler_params=pltpu.CompilerParams(vmem_limit_bytes=VMEM_LIMIT),
         name="place_gradients",
     )(tie, sums, part0, partw, part1, part2, out, grad)

time: 238 us -> 237 us (level)
  no operation moved by 1% of the time
where the time goes in v2:
time: 237 us
  Pallas kernels  236 us (100%)
    pallas_call x1, Pallas kernels, run_fused_backward(): pl.pallas_call(fused_backward, grid=(4 * groups,), in_specs=[ANY_WHOLE, A...  100 us
    pallas_call x1, Pallas kernels, run_fused_forward(): pl.pallas_call(fused_forward, grid=(groups, heads), in_specs=[SMEM_WHOLE,...  74.3 us
    pallas_call x1, Pallas kernels, run_fused_feed_forward(): pl.pallas_call(fused_feed_forward, grid=(groups,), in_specs=[SMEM_WHOLE,...  50.4 us
    pallas_call x1, Pallas kernels, run_place_gradients(): pl.pallas_call(place_gradients, grid=(slots,), in_specs=[SMEM_WHOLE] + [V...  11.2 us

profile of v2, /device:TPU:0, one launch (start us, length us, event | category | flops | bytes accessed | tf_op | source)
XLA Modules:
  0.0 236.9 jit_solution(4118968194672013043)
XLA Ops:
  0.6 74.3 %fused_forward.1 = (bf16[4,768,576]{2,1,0:T(8,128)(2,1)}, bf16[4,768,192]{2,1,0:T(8,128)(2,1)}, bf16[4,4,2,96,768]{4,3,2,1,0:T(8,128)(2,1)}, bf16[4,4,2,96,768]{...) custom-call(s32[4]{0:T(128)} %tie_ref.3, ...), custom_call_target="tpu_custom_call" | custom-call | tf_op jit(solution)/shard_map/fused_forward/pallas_call | solution.py:863
  75.0 50.4 %fused_feed_forward.1 = (bf16[1024,768]{1,0:T(8,128)(2,1)}, bf16[2,4,96,768]{3,2,1,0:T(8,128)(2,1)}, bf16[2,4,2,96,768]{4,3,2,1,0:T(8,128)(2,1)}, f32[1024,768]{...) custom-call(s32[4]{0:T(128)} %len_ref.3, bf16[4,1024,768]{2,1,0:T(8,128)(2,1)} %bitcast.10, ...), custom_call_target="tpu_custom_call" | custom-call | tf_op jit(solution)/shard_map/fused_feed_forward/pallas_call | solution.py:1172
  125.4 100.1 %fused_backward.1 = (bf16[4,1024,768]{2,1,0:T(8,128)(2,1)}, bf16[4,1024,768]{2,1,0:T(8,128)(2,1)}, f32[96,576]{1,0:T(8,128)}, f32[96,192]{1,0:T(8,128)}, f32[96,...) custom-call(bf16[4,1024,768]{2,1,0:T(8,128)(2,1)} %bitcast.9, bf16[4,768,576]{2,1,0:T(8,128)(2,1)} %get-tuple-element.45.gq_in, ...), custom_call_target="tpu_custom_call" | custom-call | tf_op jit(solution)/shard_map/fused_backward/pallas_call | solution.py:1607
  225.5 11.2 %place_gradients.1 = (bf16[4,1024,768]{2,1,0:T(8,128)(2,1)}, bf16[4,1024,768]{2,1,0:T(8,128)(2,1)}, f32[4,2,24]{2,1,0:T(2,128)}, f32[10,4,24]{2,1,0:T(4,128)}, f...) custom-call(s32[4]{0:T(128)} %tie_ref.3, ...), custom_call_target="tpu_custom_call" | custom-call | tf_op jit(solution)/shard_map/place_gradients/pallas_call | solution.py:1707
